TPU v7x, 256 devices: a whole 4x4x8 slice. The times are simulated.
256 devices in a mesh: ra: 32 (over x, z), dec: 4 (over y), band: 2 (over core).
Axes of the slice: x: 4, y: 4, z: 8, core: 2. Of those that a mesh axis runs over, the one named last changes fastest.
Arguments:
- morphology: bfloat16 [32, 4, 128, 4096], P('ra', 'dec'), may hold values from 0 to 1
- sed_amps: float32 [32, 4, 6, 128], P('ra', 'dec', 'band'), may hold values from 0.1 to 2
- slot_lists: int32 [32, 4, 5, 128], P('ra', 'dec'), may hold values from 0 to 16, as said below
- morph_step: float32 [32, 4, 128], P('ra', 'dec'), may hold values from 0.01 to 0.04
- sed_step: float32 [32, 4, 128], P('ra', 'dec'), may hold values from 9.765625e-06 to 3.90625e-05
- psf_kernels: bfloat16 [6, 32, 4096], P('band', 'ra'), may hold values from -0.75 to 0.75
- observed: bfloat16 [32, 4, 6, 16, 4096], P('ra', 'dec', 'band'), may hold values from -16 to 16
Outputs:
- morph_out: float32 [32, 4, 128, 4096], P('ra', 'dec', None, 'band')
- sed_out: float32 [32, 4, 6, 128], P('ra', 'dec', 'band')
Inputs may be any that keep to these rules, and one draw needn't show every extreme that they name: `slot_lists`: in each home tile the sources 0 to some count - 1 are live (the count at least 32, and 128 in some tile); a live source has a slot below 16 in row 0; every other entry of a dead source is 16. No source lands beyond the declination edges. Each of rows 1 to 4 of a home tile holds at most 32 entries below 16, and some tile's row 1 holds exactly 32.
All inputs are finite; a program needn't handle non-finite values.
Results may differ from a plain program's by a relative error of at most 0.015.
Values may be sent and summed in bfloat16 or wider, within the bound.
A program may use at most 256 MiB of HBM per device.

v0:
```python
import functools
import jax
import jax.numpy as jnp
from jax import lax
from jax.experimental import pallas as pl
from jax.experimental.pallas import tpu as pltpu
from jax.sharding import PartitionSpec as P

SIDE = 64
KERN = 32
ITERS = 2
SLOTS = 16
CAP = 32
SRC = 128
HALF = 2048
MESH = pl.DeviceIdType.MESH
F32 = jnp.float32
BF16 = jnp.bfloat16
I32 = jnp.int32


def lane_lo(rows):
    return lax.broadcasted_iota(I32, (rows, 128), 1) < SIDE


def swap(value):
    return pltpu.roll(value, SIDE, axis=1)


def block_diag(first, second):
    low = jnp.where(lane_lo(SIDE), 1.0, 0.0).astype(BF16)
    high = jnp.where(lane_lo(SIDE), 0.0, 1.0).astype(BF16)
    zero = jnp.zeros((SIDE, 128), BF16)
    return jnp.concatenate(
        [
            jnp.concatenate([first * low, zero], axis=1),
            jnp.concatenate([first * high, zero], axis=1),
            jnp.concatenate([zero, second], axis=1),
            jnp.concatenate([zero, zero], axis=1),
        ],
        axis=0,
    )


def dot(a, b):
    return jnp.dot(a, b, preferred_element_type=F32)


def turned(row):
    return jnp.broadcast_to(row, (SRC, SRC)).T


def places(row):
    source = lax.broadcasted_iota(I32, (1, SRC), 1)
    key_row = row * SRC + source
    column = turned(row)
    key_col = column * SRC + lax.broadcasted_iota(I32, (SRC, SRC), 0)
    rank = jnp.sum(jnp.where(key_col < key_row, 1, 0), axis=0, keepdims=True)
    below = jnp.sum(
        jnp.where(column < lax.broadcasted_iota(I32, (SRC, SRC), 1), 1, 0), axis=0, keepdims=True
    )
    return rank, below


def chosen(row, rank):
    entry = lax.broadcasted_iota(I32, (CAP, SRC), 0)
    return jnp.where(rank == entry, 1, 0) * jnp.where(row < SLOTS, 1, 0)


def to_stamps(parts, low_ref, high_ref, pair):
    x0, x1, x2 = parts
    mask = lane_lo(SLOTS)
    even, odd = pl.ds(2 * pair, SLOTS, stride=SIDE), pl.ds(2 * pair + 1, SLOTS, stride=SIDE)
    low_ref[even, :] = jnp.where(mask, x0, swap(x1))
    low_ref[odd, :] = jnp.where(mask, swap(x0), x1)
    high_ref[even, :] = jnp.where(mask, x2, 0.0)
    high_ref[odd, :] = jnp.where(mask, swap(x2), 0.0)


def deblend(
    n_ra, n_dec,
    morph, sed, lists, mstep, sstep, psf, obs,
    out_m, out_a,
    kp, k3, kt3, kst_lo, kst_hi,
    lists8, lists_in, amps, amps_in, amp_now,
    pick_out, pick_back, home_amp, home_back, step_col, entries, table,
    mq, mf, vout, vin, xs, s_lo, s_hi, o_lo, o_hi, zs, pfx, model, resid,
    b_lo, b_hi, bflat, gs, gflat, gsum, gin, gret, hown, hsend, hin,
    arep, ga_rows, ga_send, ga_ret, ga_home,
    psf_send, psf_recv, list_sem, amp_sem, vis_sem, fwd_sem, mine_sem, home_sem,
    part_sem, back_sem, gain_sem, table_sem,
):
    r = lax.axis_index("ra")
    c = lax.axis_index("dec")
    b = lax.axis_index("band")
    other = 1 - b
    right, left = lax.rem(r + 1, n_ra), lax.rem(r + n_ra - 1, n_ra)
    up, down = lax.rem(c + 1, n_dec), lax.rem(c + n_dec - 1, n_dec)
    target = [(right, c, b), (left, c, b), (r, up, b), (r, down, b)]
    origin = [(left, c, b), (right, c, b), (r, down, b), (r, up, b)]
    sibling = (r, c, other)
    nk = min(SLOTS, n_ra)

    def send(src, dst, sems, index, device):
        return pltpu.make_async_remote_copy(
            src_ref=src, dst_ref=dst,
            send_sem=sems.at[(0,) + index], recv_sem=sems.at[(1,) + index],
            device_id=device, device_id_type=MESH,
        )

    barrier = pltpu.get_barrier_semaphore()

    def greet(step, carry):
        pl.semaphore_signal(
            barrier, inc=1, device_id=(lax.rem(r + step, n_ra), c, b), device_id_type=MESH
        )
        return carry

    lax.fori_loop(1, n_ra, greet, 0)
    for device in target[2:] + [sibling]:
        pl.semaphore_signal(barrier, inc=1, device_id=device, device_id_type=MESH)
    lists8[...] = jnp.full((8, SRC), SLOTS, I32)
    lists8[0:5, :] = lists[...]
    amp_now[...] = jnp.zeros((8, SRC), F32)
    amp_now[0:3, :] = sed[...]
    amps[0] = amp_now[...].astype(BF16).astype(F32)
    pl.semaphore_wait(barrier, n_ra - 1 + 3)

    list_copies = [
        send(lists8, lists_in.at[d], list_sem, (d,), target[d]) for d in range(4)
    ]
    for copy in list_copies:
        copy.start()

    def psf_copy(step):
        return pltpu.make_async_remote_copy(
            src_ref=psf, dst_ref=kp.at[lax.rem(r, SLOTS)],
            send_sem=psf_send.at[step], recv_sem=psf_recv.at[lax.rem(r, SLOTS)],
            device_id=(lax.rem(r + step, n_ra), c, b), device_id_type=MESH,
        )

    def spread_psf():
        def body(step, carry):
            psf_copy(step).start()
            return carry

        lax.fori_loop(1, n_ra, body, 0)
        kp[lax.rem(r, SLOTS)] = psf[...]

    def amp_copy(it, d):
        return send(amps.at[it], amps_in.at[it, d], amp_sem, (it, d), target[d])

    def vis_copy(it, d):
        rows = pl.ds(CAP * d, CAP)
        return send(vout.at[it, rows], vin.at[it, b, rows], vis_sem, (it, d), target[d])

    def fwd_copy(it, d, half):
        rows = pl.ds(CAP * d, CAP)
        return send(vin.at[it, half, rows], vin.at[it, half, rows], fwd_sem, (it, d), sibling)

    def mine_copy(half):
        return send(mq.at[1, half], mq.at[1, half], mine_sem, (0,), sibling)

    def home_copy(it):
        return send(hsend.at[it], hin.at[it], home_sem, (it,), sibling)

    def part_copy(it, d, half):
        rows = pl.ds(CAP * d, CAP)
        return send(gflat.at[it, half, rows], gin.at[it, rows], part_sem, (it, d), sibling)

    def back_copy(it, d):
        rows = pl.ds(CAP * d, CAP)
        return send(gsum.at[it, rows], gret.at[it, rows], back_sem, (it, d), origin[d])

    def gain_copy(it, d):
        return send(ga_send.at[it], ga_ret.at[it, d], gain_sem, (it, d), origin[d])

    for d in range(4):
        amp_copy(0, d).start()

    for d in range(4):
        row = lists8[d + 1 : d + 2, :]
        rank, _ = places(row)
        entries[pl.ds(CAP * d, CAP), :] = chosen(row, rank)
    pick = entries[...].astype(F32)
    pick_out[...] = pick
    pick_back[...] = pick.T.astype(BF16)

    mq[0, 0] = morph[:, 0:HALF]
    mq[0, 1] = morph[:, HALF : 2 * HALF]
    mf[...] = mq[0, b].astype(F32)

    def send_visitors(it):
        def body(j, carry):
            cols = pl.ds(pl.multiple_of(j * 256, 256), 256)
            vout[it, :, cols] = dot(pick_out[...].astype(BF16), mq[it, b, :, cols]).astype(BF16)
            return carry

        lax.fori_loop(0, HALF // 256, body, 0)
        for d in range(4):
            vis_copy(it, d).start()

    send_visitors(0)

    @pl.when(r < SLOTS)
    def _():
        spread_psf()

    if nk < SLOTS:
        kp[nk:SLOTS] = jnp.zeros((SLOTS - nk, 96, 128), BF16)

    step_col[...] = turned(mstep[...])
    slot0 = lists8[0:1, :]
    is_slot = jnp.where(slot0 == lax.broadcasted_iota(I32, (SLOTS, SRC), 0), 1.0, 0.0)
    bflat[...] = jnp.zeros(bflat.shape, BF16)
    pfx[0] = jnp.zeros((SIDE, 256), F32)
    pfx[65] = jnp.zeros((SIDE, 256), F32)

    for half in range(2):
        def obs_body(j, carry, half=half):
            cols = pl.ds(pl.multiple_of((half * 16 + j) * 128, 128), 128)
            parts = [obs[band, :, cols].astype(F32) for band in range(3)]
            to_stamps(parts, o_lo, o_hi, half * 16 + j)
            return carry

        lax.fori_loop(0, 16, obs_body, 0)

    def take_lists():
        table[...] = jnp.zeros((8, SRC), I32)
        for d in range(4):
            list_copies[d].wait_recv()
            row = lists_in[d, d + 1 : d + 2, :]
            rank, below = places(row)
            picked = chosen(row, rank)
            entries[pl.ds(CAP * d, CAP), :] = picked
            table[d + 2 : d + 3, :] = jnp.minimum(below, CAP)
        first, second = [], []
        for d in range(4):
            picked = entries[pl.ds(CAP * d, CAP), :]
            first.append(picked * lists_in[d, 0:1, :])
            second.append(picked * lists_in[d, d + 1 : d + 2, :])
        table[0:1, :] = jnp.minimum(
            jnp.sum(jnp.concatenate(first, axis=0).T, axis=0, keepdims=True), SLOTS - 1
        )
        table[1:2, :] = jnp.minimum(
            jnp.sum(jnp.concatenate(second, axis=0).T, axis=0, keepdims=True), SLOTS - 1
        )

    take_lists()

    def with_table(smem):
        copy = pltpu.make_async_copy(table, smem, table_sem)
        copy.start()
        copy.wait()
        for it in range(ITERS):
            one_iteration(it, smem)

    def home_weights(it):
        rows = [is_slot * amps[it, band : band + 1, :] for band in range(3)]
        full = jnp.concatenate(rows + [jnp.zeros((SRC - 48, SRC), F32)], axis=0)
        home_amp[...] = full[0:48].astype(BF16)
        home_back[...] = full.T.astype(BF16)

    def unpack(k):
        mask = lane_lo(SIDE)
        p01 = kp[k, 0:SIDE, :].astype(F32)
        fold = kp[k, SIDE:96, :].astype(F32)
        mask32 = lane_lo(32)
        p2 = jnp.concatenate(
            [jnp.where(mask32, fold, 0.0), jnp.where(mask32, swap(fold), 0.0)], axis=0
        )
        flip = jnp.concatenate([p01, p2], axis=0).T
        u, w = flip[0:SIDE], flip[SIDE:128]
        k3[k, :, 0:128] = p01.astype(BF16)
        k3[k, :, 128:256] = p2.astype(BF16)
        kt3[k, :, 0:128] = jnp.where(mask, u, swap(w)).astype(BF16)
        kt3[k, :, 128:256] = jnp.where(mask, swap(u), 0.0).astype(BF16)
        zero = jnp.zeros((SIDE, 128), BF16)
        p01s = swap(p01)
        kst_lo[k, 0:64, :] = jnp.where(mask, p01, 0.0).astype(BF16)
        kst_lo[k, 64:128, :] = jnp.where(mask, p01s, 0.0).astype(BF16)
        kst_lo[k, 128:192, :] = p2.astype(BF16)
        kst_lo[k, 192:256, :] = zero
        kst_hi[k, 0:64, :] = jnp.where(mask, 0.0, p01s).astype(BF16)
        kst_hi[k, 64:128, :] = jnp.where(mask, 0.0, p01).astype(BF16)
        kst_hi[k, 128:192, :] = swap(p2).astype(BF16)
        kst_hi[k, 192:256, :] = zero

    def one_iteration(it, smem):
        home_weights(it)

        for half in range(2):
            def sum_body(j, carry, half=half):
                cols = pl.ds(pl.multiple_of(j * 128, 128), 128)
                x = dot(home_amp[...], mq[it, half, :, cols])
                to_stamps([x[0:16], x[16:32], x[32:48]], s_lo, s_hi, half * 16 + j)
                return carry

            lax.fori_loop(0, 16, sum_body, 0)

        def home_model(q, carry):
            if it == 0:
                @pl.when(jnp.logical_and(q != r, q < nk))
                def _():
                    pltpu.make_async_remote_copy(
                        src_ref=psf, dst_ref=kp.at[q], send_sem=psf_send.at[0],
                        recv_sem=psf_recv.at[q], device_id=sibling, device_id_type=MESH,
                    ).wait_recv()

                unpack(q)
            rows = pl.ds(pl.multiple_of(q * SIDE, SIDE), SIDE)
            s = jnp.concatenate([s_lo[rows, :], s_hi[rows, :]], axis=1).astype(BF16)
            kt = kt3[q]
            z = dot(s, block_diag(kt[:, 0:128], kt[:, 128:256])).astype(BF16)
            model[q] = dot(k3[q], block_diag(z[:, 0:128], z[:, 128:256]))
            return carry

        lax.fori_loop(0, SLOTS, home_model, 0)

        for d in range(4):
            amp_copy(it, d).wait_recv()
            picked = entries[pl.ds(CAP * d, CAP), :].astype(F32)
            cols = [
                jnp.sum(picked * amps_in[it, d, band : band + 1, :], axis=1, keepdims=True)
                for band in range(3)
            ]
            mask = lane_lo(CAP)
            rows = pl.ds(CAP * d, CAP)
            arep[rows, 0:128] = jnp.where(mask, cols[0], cols[1])
            arep[rows, 128:256] = jnp.where(mask, cols[2], 0.0)

        for d in range(4):
            vis_copy(it, d).wait_recv()
            fwd_copy(it, d, b).start()
        for d in range(4):
            fwd_copy(it, d, other).wait_recv()
        for half in range(2):
            def stamp_body(j, carry, half=half):
                cols = pl.ds(pl.multiple_of(j * 128, 128), 128)
                mask = lane_lo(64)
                xa = vin[it, half, 0:64, cols].astype(F32)
                xb = vin[it, half, 64:128, cols].astype(F32)
                pair = half * 16 + j
                xs[pl.ds(2 * pair, 64, stride=SIDE), :] = jnp.where(mask, xa, swap(xb))
                xs[pl.ds(2 * pair + 1, 64, stride=SIDE), :] = jnp.where(mask, swap(xa), xb)
                return carry

            lax.fori_loop(0, 16, stamp_body, 0)

        unroll = 4

        def visit_model(step, carry):
            acc = list(carry)
            blank = jnp.zeros((SIDE, 256), BF16)
            for u in range(unroll):
                p = step * unroll + u
                x = xs[pl.ds(pl.multiple_of(p * SIDE, SIDE), SIDE), :].astype(BF16)
                for side in range(2):
                    v = p + 64 * side
                    k = smem[0, v]
                    kt = kt3[k]
                    weights = jnp.concatenate([kt, blank] if side == 0 else [blank, kt], axis=0)
                    z = dot(x, weights).astype(BF16)
                    zs[v] = z
                    conv = dot(k3[k], block_diag(z[:, 0:128], z[:, 128:256]))
                    acc[side] = acc[side] + conv * arep[pl.ds(v, 1), :]
                    pfx[65 * side + p + 1] = acc[side]
            return tuple(acc)

        start = jnp.zeros((SIDE, 256), F32)
        lax.fori_loop(0, 64 // unroll, visit_model, (start, start))

        def home_back_body(q, carry):
            total = model[q]
            for d in range(4):
                base = (0, 32, 65, 97)[d]
                total = total + (pfx[base + smem[d + 2, q + 1]] - pfx[base + smem[d + 2, q]])
            rows = pl.ds(pl.multiple_of(q * SIDE, SIDE), SIDE)
            seen = jnp.concatenate([o_lo[rows, :], o_hi[rows, :]], axis=1)
            res = (total - seen).astype(BF16)
            diag = block_diag(res[:, 0:128], res[:, 128:256])
            resid[q] = diag
            t = dot(kt3[q], diag).astype(BF16)
            kk = k3[q]
            back = dot(t, block_diag(kk[:, 0:128], kk[:, 128:256]))
            b_lo[rows, :] = back[:, 0:128]
            b_hi[rows, :] = back[:, 128:256]
            return carry

        lax.fori_loop(0, SLOTS, home_back_body, 0)

        for half in range(2):
            def flat_body(j, carry, half=half):
                pair = half * 16 + j
                mask = lane_lo(SLOTS)
                even = pl.ds(2 * pair, SLOTS, stride=SIDE)
                odd = pl.ds(2 * pair + 1, SLOTS, stride=SIDE)
                e0, o0, e2, o2 = b_lo[even, :], b_lo[odd, :], b_hi[even, :], b_hi[odd, :]
                x = jnp.concatenate(
                    [
                        jnp.where(mask, e0, swap(o0)),
                        jnp.where(mask, swap(e0), o0),
                        jnp.where(mask, e2, swap(o2)),
                    ],
                    axis=0,
                )
                bflat[half, 0:48, pl.ds(pl.multiple_of(j * 128, 128), 128)] = x.astype(BF16)
                return carry

            lax.fori_loop(0, 16, flat_body, 0)

        def home_grad(j, carry):
            cols = pl.ds(pl.multiple_of(j * 256, 256), 256)
            hsend[it, :, cols] = dot(home_back[...], bflat[other, :, cols]).astype(BF16)
            hown[:, cols] = dot(home_back[...], bflat[b, :, cols])
            return carry

        lax.fori_loop(0, HALF // 256, home_grad, 0)
        home_copy(it).start()

        def home_gain(j, carry):
            cols = pl.ds(pl.multiple_of(j * 256, 256), 256)
            for half in range(2):
                carry = carry + lax.dot_general(
                    bflat[half, 0:48, cols], mq[it, half, :, cols], (((1,), (1,)), ((), ())),
                    preferred_element_type=F32,
                )
            return carry

        gain = lax.fori_loop(0, HALF // 256, home_gain, jnp.zeros((48, SRC), F32))
        ga_home[...] = jnp.concatenate(
            [
                jnp.sum(is_slot * gain[16 * band : 16 * band + 16], axis=0, keepdims=True)
                for band in range(3)
            ]
            + [jnp.zeros((5, SRC), F32)],
            axis=0,
        )

        def visit_back(step, carry):
            for u in range(unroll):
                p = step * unroll + u
                scaled, weights = [], []
                for side in range(2):
                    v = p + 64 * side
                    k = smem[0, v]
                    t = dot(kt3[k], resid[smem[1, v]])
                    ga_rows[pl.ds(v, 1), :] = jnp.sum(t * zs[v].astype(F32), axis=0, keepdims=True)
                    scaled.append((t * arep[pl.ds(v, 1), :]).astype(BF16))
                    weights.append(kst_lo[k] if side == 0 else kst_hi[k])
                gs[pl.ds(pl.multiple_of(p * SIDE, SIDE), SIDE), :] = dot(
                    scaled[0], weights[0]
                ) + dot(scaled[1], weights[1])
            return carry

        lax.fori_loop(0, 64 // unroll, visit_back, 0)

        for half in range(2):
            def grad_body(j, carry, half=half):
                pair = half * 16 + j
                mask = lane_lo(64)
                e = gs[pl.ds(2 * pair, 64, stride=SIDE), :]
                o = gs[pl.ds(2 * pair + 1, 64, stride=SIDE), :]
                cols = pl.ds(pl.multiple_of(j * 128, 128), 128)
                gflat[it, half, 0:64, cols] = jnp.where(mask, e, swap(o)).astype(BF16)
                gflat[it, half, 64:128, cols] = jnp.where(mask, swap(e), o).astype(BF16)
                return carry

            lax.fori_loop(0, 16, grad_body, 0)
        for d in range(4):
            part_copy(it, d, other).start()
        select = jnp.where(
            lax.broadcasted_iota(I32, (8, 256), 1) // SIDE
            == lax.broadcasted_iota(I32, (8, 256), 0),
            1.0,
            0.0,
        )
        ga_send[it] = lax.dot_general(
            select, ga_rows[...], (((1,), (1,)), ((), ())),
            preferred_element_type=F32, precision=lax.Precision.HIGHEST,
        )
        for d in range(4):
            gain_copy(it, d).start()
        for d in range(4):
            part_copy(it, d, other).wait_recv()
            rows = pl.ds(CAP * d, CAP)
            gsum[it, rows, :] = (
                gflat[it, b, rows, :].astype(F32) + gin[it, rows, :].astype(F32)
            ).astype(BF16)
            back_copy(it, d).start()

        lane = lax.broadcasted_iota(I32, (8, SRC), 1) // CAP
        returned = jnp.zeros((8, SRC), F32)
        for d in range(4):
            gain_copy(it, d).wait_recv()
            returned = returned + jnp.where(lane == d, ga_ret[it, d], 0.0)
        gain = ga_home[...] + jnp.dot(
            returned, pick_out[...], preferred_element_type=F32, precision=lax.Precision.HIGHEST
        )
        amp_now[...] = jnp.maximum(amp_now[...] - sstep[...] * gain, 0.0)
        if it == 0:
            amps[1] = amp_now[...].astype(BF16).astype(F32)
            for d in range(4):
                amp_copy(1, d).start()
        else:
            out_a[...] = amp_now[0:3, :]
        home_copy(it).wait_recv()
        for d in range(4):
            back_copy(it, d).wait_recv()

        def update(j, carry):
            cols = pl.ds(pl.multiple_of(j * 128, 128), 128)
            grad = hown[:, cols] + hin[it, :, cols].astype(F32)
            grad = grad + dot(pick_back[...], gret[it, :, cols])
            fresh = jnp.maximum(mf[:, cols] - step_col[...] * grad, 0.0)
            if it == 0:
                mf[:, cols] = fresh
                mq[1, b, :, cols] = fresh.astype(BF16)
            else:
                out_m[:, cols] = fresh
            return carry

        lax.fori_loop(0, HALF // 128, update, 0)
        if it == 0:
            send_visitors(1)
            mine_copy(b).start()
            mine_copy(other).wait_recv()

    pl.run_scoped(with_table, pltpu.SMEM((8, SRC), I32))

    for copy in list_copies:
        copy.wait_send()
    mine_copy(b).wait_send()
    for it in range(ITERS):
        home_copy(it).wait_send()
        for d in range(4):
            amp_copy(it, d).wait_send()
            vis_copy(it, d).wait_send()
            fwd_copy(it, d, b).wait_send()
            part_copy(it, d, other).wait_send()
            back_copy(it, d).wait_send()
            gain_copy(it, d).wait_send()

    @pl.when(r < SLOTS)
    def _():
        def body(step, carry):
            psf_copy(step).wait_send()
            return carry

        lax.fori_loop(1, n_ra, body, 0)


def shards(morphology, sed_amps, slot_lists, morph_step, sed_step, psf_kernels, observed):
    n_ra, n_dec = lax.axis_size("ra"), lax.axis_size("dec")
    kernels = psf_kernels.reshape(3, SIDE, SIDE)
    packed = jnp.concatenate(
        [
            jnp.concatenate([kernels[0], kernels[1]], axis=1),
            jnp.concatenate([kernels[2, :32], kernels[2, 32:]], axis=1),
        ],
        axis=0,
    )
    vmem = pl.BlockSpec(memory_space=pltpu.VMEM)
    dma = pltpu.SemaphoreType.DMA
    scratch = [
        pltpu.VMEM((SLOTS, 96, 128), BF16),
        pltpu.VMEM((SLOTS, SIDE, 256), BF16),
        pltpu.VMEM((SLOTS, SIDE, 256), BF16),
        pltpu.VMEM((SLOTS, 256, 128), BF16),
        pltpu.VMEM((SLOTS, 256, 128), BF16),
        pltpu.VMEM((8, SRC), I32),
        pltpu.VMEM((4, 8, SRC), I32),
        pltpu.VMEM((2, 8, SRC), F32),
        pltpu.VMEM((2, 4, 8, SRC), F32),
        pltpu.VMEM((8, SRC), F32),
        pltpu.VMEM((SRC, SRC), F32),
        pltpu.VMEM((SRC, SRC), BF16),
        pltpu.VMEM((48, SRC), BF16),
        pltpu.VMEM((SRC, SRC), BF16),
        pltpu.VMEM((SRC, SRC), F32),
        pltpu.VMEM((SRC, SRC), I32),
        pltpu.VMEM((8, SRC), I32),
        pltpu.VMEM((2, 2, SRC, HALF), BF16),
        pltpu.VMEM((SRC, HALF), F32),
        pltpu.VMEM((2, SRC, HALF), BF16),
        pltpu.VMEM((2, 2, SRC, HALF), BF16),
        pltpu.VMEM((64 * SIDE, 128), F32),
        pltpu.VMEM((SLOTS * SIDE, 128), F32),
        pltpu.VMEM((SLOTS * SIDE, 128), F32),
        pltpu.VMEM((SLOTS * SIDE, 128), F32),
        pltpu.VMEM((SLOTS * SIDE, 128), F32),
        pltpu.VMEM((SRC, SIDE, 256), BF16),
        pltpu.VMEM((130, SIDE, 256), F32),
        pltpu.VMEM((SLOTS, SIDE, 256), F32),
        pltpu.VMEM((SLOTS, 256, 256), BF16),
        pltpu.VMEM((SLOTS * SIDE, 128), F32),
        pltpu.VMEM((SLOTS * SIDE, 128), F32),
        pltpu.VMEM((2, SRC, HALF), BF16),
        pltpu.VMEM((64 * SIDE, 128), F32),
        pltpu.VMEM((2, 2, SRC, HALF), BF16),
        pltpu.VMEM((2, SRC, HALF), BF16),
        pltpu.VMEM((2, SRC, HALF), BF16),
        pltpu.VMEM((2, SRC, HALF), BF16),
        pltpu.VMEM((SRC, HALF), F32),
        pltpu.VMEM((2, SRC, HALF), BF16),
        pltpu.VMEM((2, SRC, HALF), BF16),
        pltpu.VMEM((SRC, 256), F32),
        pltpu.VMEM((SRC, 256), F32),
        pltpu.VMEM((2, 8, SRC), F32),
        pltpu.VMEM((2, 4, 8, SRC), F32),
        pltpu.VMEM((8, SRC), F32),
        dma((n_ra,)), dma((SLOTS,)),
        dma((2, 4)), dma((2, 2, 4)), dma((2, 2, 4)), dma((2, 2, 4)), dma((2, 1)), dma((2, 2)),
        dma((2, 2, 4)), dma((2, 2, 4)), dma((2, 2, 4)), dma,
    ]
    out_m, out_a = pl.pallas_call(
        functools.partial(deblend, n_ra, n_dec),
        out_shape=(
            jax.ShapeDtypeStruct((SRC, HALF), F32),
            jax.ShapeDtypeStruct((3, SRC), F32),
        ),
        in_specs=[vmem] * 7,
        out_specs=(vmem, vmem),
        scratch_shapes=scratch,
        compiler_params=pltpu.CompilerParams(
            collective_id=0, has_side_effects=True, vmem_limit_bytes=60 * 1024 * 1024
        ),
        name="deblend",
    )(
        morphology[0, 0], sed_amps[0, 0], slot_lists[0, 0], morph_step[0], sed_step[0],
        packed, observed[0, 0],
    )
    return out_m[None, None], out_a[None, None]


def solution(mesh):
    in_specs = (
        P("ra", "dec", None, None),
        P("ra", "dec", "band", None),
        P("ra", "dec", None, None),
        P("ra", "dec", None),
        P("ra", "dec", None),
        P("band", "ra", None),
        P("ra", "dec", "band", None, None),
    )
    out_specs = (P("ra", "dec", None, "band"), P("ra", "dec", "band", None))
    return jax.shard_map(shards, mesh=mesh, in_specs=in_specs, out_specs=out_specs, check_vma=False)
```

profile of v0, /device:TPU:1, one launch (start us, length us, event | category | flops | bytes accessed | tf_op | source)
XLA Modules:
  0.0 183.1 jit_solution(12251235311228459536)
XLA Ops:
  0.6 0.0 copy-start.3
  0.6 0.7 copy-done.3
  1.3 0.0 copy-start.1
  1.3 0.6 copy.15
  1.9 0.1 copy-done.1
  2.0 0.6 copy.14
  2.6 0.9 slice_reduce_fusion.1
  3.5 0.0 copy-start
  3.5 0.1 squeeze.35
  3.6 0.1 squeeze.36
  3.7 0.6 copy-done
  4.3 0.1 reshape.11
  4.4 0.7 maximum_maximum_fusion.psf
  5.1 174.4 %deblend.1 = (f32[128,2048]{1,0:T(8,128)}, f32[3,128]{1,0:T(4,128)}) custom-call(bf16[128,4096]{1,0:T(8,128)(2,1)} %bitcast.18, f32[3,128]{1,0:T(4,128)} %bitcast.22, s32[5,128]{1,0:T(8,128)} %bitcast.21, f32[1,128]{1,0:T(1,128)} %bitcast.24, f32[1,128]{1,0:T(1,128)} %bitcast.25, bf16[96,128]{1,0:T(8,128)(2,1)} %maximum_maximum_fusion.psf, ...), custom_call_target="tpu_custom_call" | custom-call | tf_op jit(solution)/shard_map/deblend/pallas_call | solution.py:616
  179.5 0.0 copy-start.2
  179.5 0.7 copy-done.2
  180.2 0.6 copy.9
  180.8 2.3 %copy.17 = f32[1,1,128,2048]{3,2,1,0:T(8,128)} copy(f32[1,1,128,2048]{3,2,1,0:T(8,128)} %bitcast.19) | data formatting | bytes 2097152
  (1 shorter events, 0.0 us)
Async XLA Ops:
  0.6 0.7 copy-start.3
  1.3 0.7 copy-start.1
  3.5 0.8 copy-start
  179.5 0.7 copy-start.2
where the time goes:
time: 183 us
  Pallas kernels  174 us (95%)
  local copies, waits for them, and re-layouts  7.26 us (4%)
    pallas_call x1, Pallas kernels, shards(): pl.pallas_call(functools.partial(deblend, n_ra, n_dec), out_shape=(jax.Sh...  174 us
    unnamed x12, local copies, waits for them, and re-layouts  6.06 us

commit v1 on v0

--- a/solution.py
+++ b/solution.py
@@ -13,6 +13,10 @@
 CAP = 32
 SRC = 128
 HALF = 2048
+PITCH = 72
+ROWS = 8
+HOME = 8
+PAIRS = 8
 MESH = pl.DeviceIdType.MESH
 F32 = jnp.float32
 BF16 = jnp.bfloat16
@@ -46,6 +50,15 @@
     return jnp.dot(a, b, preferred_element_type=F32)
 
 
+def tiled(count, unroll, body):
+    def steps(step, carry):
+        for u in range(unroll):
+            body(step * unroll + u, carry)
+        return carry
+
+    lax.fori_loop(0, count // unroll, steps, 0)
+
+
 def turned(row):
     return jnp.broadcast_to(row, (SRC, SRC)).T
 
@@ -70,7 +83,7 @@
 def to_stamps(parts, low_ref, high_ref, pair):
     x0, x1, x2 = parts
     mask = lane_lo(SLOTS)
-    even, odd = pl.ds(2 * pair, SLOTS, stride=SIDE), pl.ds(2 * pair + 1, SLOTS, stride=SIDE)
+    even, odd = pl.ds(2 * pair, SLOTS, stride=PITCH), pl.ds(2 * pair + 1, SLOTS, stride=PITCH)
     low_ref[even, :] = jnp.where(mask, x0, swap(x1))
     low_ref[odd, :] = jnp.where(mask, swap(x0), x1)
     high_ref[even, :] = jnp.where(mask, x2, 0.0)
@@ -223,7 +236,7 @@
             to_stamps(parts, o_lo, o_hi, half * 16 + j)
             return carry
 
-        lax.fori_loop(0, 16, obs_body, 0)
+        tiled(16, ROWS, obs_body)
 
     def take_lists():
         table[...] = jnp.zeros((8, SRC), I32)
@@ -296,10 +309,10 @@
                 to_stamps([x[0:16], x[16:32], x[32:48]], s_lo, s_hi, half * 16 + j)
                 return carry
 
-            lax.fori_loop(0, 16, sum_body, 0)
-
-        def home_model(q, carry):
-            if it == 0:
+            tiled(16, ROWS, sum_body)
+
+        if it == 0:
+            def ready(q, carry):
                 @pl.when(jnp.logical_and(q != r, q < nk))
                 def _():
                     pltpu.make_async_remote_copy(
@@ -307,15 +320,29 @@
                         recv_sem=psf_recv.at[q], device_id=sibling, device_id_type=MESH,
                     ).wait_recv()
 
+                return carry
+
+            lax.fori_loop(0, SLOTS, ready, 0)
+
+            def unpack_body(q, carry):
                 unpack(q)
-            rows = pl.ds(pl.multiple_of(q * SIDE, SIDE), SIDE)
-            s = jnp.concatenate([s_lo[rows, :], s_hi[rows, :]], axis=1).astype(BF16)
-            kt = kt3[q]
-            z = dot(s, block_diag(kt[:, 0:128], kt[:, 128:256])).astype(BF16)
-            model[q] = dot(k3[q], block_diag(z[:, 0:128], z[:, 128:256]))
-            return carry
-
-        lax.fori_loop(0, SLOTS, home_model, 0)
+                return carry
+
+            tiled(SLOTS, 4, unpack_body)
+
+        def home_model(step, carry):
+            slots = [step * HOME + u for u in range(HOME)]
+            z = []
+            for q in slots:
+                rows = pl.ds(pl.multiple_of(q * PITCH, 8), SIDE)
+                s = jnp.concatenate([s_lo[rows, :], s_hi[rows, :]], axis=1).astype(BF16)
+                kt = kt3[q]
+                z.append(dot(s, block_diag(kt[:, 0:128], kt[:, 128:256])).astype(BF16))
+            for q, zq in zip(slots, z):
+                model[q] = dot(k3[q], block_diag(zq[:, 0:128], zq[:, 128:256]))
+            return carry
+
+        lax.fori_loop(0, SLOTS // HOME, home_model, 0)
 
         for d in range(4):
             amp_copy(it, d).wait_recv()
@@ -341,60 +368,67 @@
                 xa = vin[it, half, 0:64, cols].astype(F32)
                 xb = vin[it, half, 64:128, cols].astype(F32)
                 pair = half * 16 + j
-                xs[pl.ds(2 * pair, 64, stride=SIDE), :] = jnp.where(mask, xa, swap(xb))
-                xs[pl.ds(2 * pair + 1, 64, stride=SIDE), :] = jnp.where(mask, swap(xa), xb)
+                xs[pl.ds(2 * pair, 64, stride=PITCH), :] = jnp.where(mask, xa, swap(xb))
+                xs[pl.ds(2 * pair + 1, 64, stride=PITCH), :] = jnp.where(mask, swap(xa), xb)
                 return carry
 
-            lax.fori_loop(0, 16, stamp_body, 0)
-
-        unroll = 4
+            tiled(16, ROWS, stamp_body)
 
         def visit_model(step, carry):
             acc = list(carry)
             blank = jnp.zeros((SIDE, 256), BF16)
-            for u in range(unroll):
-                p = step * unroll + u
-                x = xs[pl.ds(pl.multiple_of(p * SIDE, SIDE), SIDE), :].astype(BF16)
+            pairs = [step * PAIRS + u for u in range(PAIRS)]
+            which = [[smem[0, p + 64 * side] for side in range(2)] for p in pairs]
+            z = []
+            for p, ks in zip(pairs, which):
+                x = xs[pl.ds(pl.multiple_of(p * PITCH, 8), SIDE), :].astype(BF16)
+                for side in range(2):
+                    kt = kt3[ks[side]]
+                    weights = jnp.concatenate([kt, blank] if side == 0 else [blank, kt], axis=0)
+                    z.append(dot(x, weights).astype(BF16))
+            for u, (p, ks) in enumerate(zip(pairs, which)):
                 for side in range(2):
                     v = p + 64 * side
-                    k = smem[0, v]
-                    kt = kt3[k]
-                    weights = jnp.concatenate([kt, blank] if side == 0 else [blank, kt], axis=0)
-                    z = dot(x, weights).astype(BF16)
-                    zs[v] = z
-                    conv = dot(k3[k], block_diag(z[:, 0:128], z[:, 128:256]))
+                    zv = z[2 * u + side]
+                    zs[v] = zv
+                    conv = dot(k3[ks[side]], block_diag(zv[:, 0:128], zv[:, 128:256]))
                     acc[side] = acc[side] + conv * arep[pl.ds(v, 1), :]
                     pfx[65 * side + p + 1] = acc[side]
             return tuple(acc)
 
         start = jnp.zeros((SIDE, 256), F32)
-        lax.fori_loop(0, 64 // unroll, visit_model, (start, start))
-
-        def home_back_body(q, carry):
-            total = model[q]
-            for d in range(4):
-                base = (0, 32, 65, 97)[d]
-                total = total + (pfx[base + smem[d + 2, q + 1]] - pfx[base + smem[d + 2, q]])
-            rows = pl.ds(pl.multiple_of(q * SIDE, SIDE), SIDE)
-            seen = jnp.concatenate([o_lo[rows, :], o_hi[rows, :]], axis=1)
-            res = (total - seen).astype(BF16)
-            diag = block_diag(res[:, 0:128], res[:, 128:256])
-            resid[q] = diag
-            t = dot(kt3[q], diag).astype(BF16)
-            kk = k3[q]
-            back = dot(t, block_diag(kk[:, 0:128], kk[:, 128:256]))
-            b_lo[rows, :] = back[:, 0:128]
-            b_hi[rows, :] = back[:, 128:256]
-            return carry
-
-        lax.fori_loop(0, SLOTS, home_back_body, 0)
+        lax.fori_loop(0, 64 // PAIRS, visit_model, (start, start))
+
+        def home_back_body(step, carry):
+            slots = [step * HOME + u for u in range(HOME)]
+            diags = []
+            for q in slots:
+                total = model[q]
+                for d in range(4):
+                    base = (0, 32, 65, 97)[d]
+                    total = total + (pfx[base + smem[d + 2, q + 1]] - pfx[base + smem[d + 2, q]])
+                rows = pl.ds(pl.multiple_of(q * PITCH, 8), SIDE)
+                seen = jnp.concatenate([o_lo[rows, :], o_hi[rows, :]], axis=1)
+                res = (total - seen).astype(BF16)
+                diags.append(block_diag(res[:, 0:128], res[:, 128:256]))
+                resid[q] = diags[-1]
+            turns = [dot(kt3[q], diag).astype(BF16) for q, diag in zip(slots, diags)]
+            for q, t in zip(slots, turns):
+                rows = pl.ds(pl.multiple_of(q * PITCH, 8), SIDE)
+                kk = k3[q]
+                back = dot(t, block_diag(kk[:, 0:128], kk[:, 128:256]))
+                b_lo[rows, :] = back[:, 0:128]
+                b_hi[rows, :] = back[:, 128:256]
+            return carry
+
+        lax.fori_loop(0, SLOTS // HOME, home_back_body, 0)
 
         for half in range(2):
             def flat_body(j, carry, half=half):
                 pair = half * 16 + j
                 mask = lane_lo(SLOTS)
-                even = pl.ds(2 * pair, SLOTS, stride=SIDE)
-                odd = pl.ds(2 * pair + 1, SLOTS, stride=SIDE)
+                even = pl.ds(2 * pair, SLOTS, stride=PITCH)
+                odd = pl.ds(2 * pair + 1, SLOTS, stride=PITCH)
                 e0, o0, e2, o2 = b_lo[even, :], b_lo[odd, :], b_hi[even, :], b_hi[odd, :]
                 x = jnp.concatenate(
                     [
@@ -407,7 +441,7 @@
                 bflat[half, 0:48, pl.ds(pl.multiple_of(j * 128, 128), 128)] = x.astype(BF16)
                 return carry
 
-            lax.fori_loop(0, 16, flat_body, 0)
+            tiled(16, ROWS, flat_body)
 
         def home_grad(j, carry):
             cols = pl.ds(pl.multiple_of(j * 256, 256), 256)
@@ -415,7 +449,7 @@
             hown[:, cols] = dot(home_back[...], bflat[b, :, cols])
             return carry
 
-        lax.fori_loop(0, HALF // 256, home_grad, 0)
+        tiled(8, 4, home_grad)
         home_copy(it).start()
 
         def home_gain(j, carry):
@@ -438,35 +472,35 @@
         )
 
         def visit_back(step, carry):
-            for u in range(unroll):
-                p = step * unroll + u
-                scaled, weights = [], []
+            pairs = [step * PAIRS + u for u in range(PAIRS)]
+            which = [[smem[0, p + 64 * side] for side in range(2)] for p in pairs]
+            scaled = []
+            for p, ks in zip(pairs, which):
                 for side in range(2):
                     v = p + 64 * side
-                    k = smem[0, v]
-                    t = dot(kt3[k], resid[smem[1, v]])
+                    t = dot(kt3[ks[side]], resid[smem[1, v]])
                     ga_rows[pl.ds(v, 1), :] = jnp.sum(t * zs[v].astype(F32), axis=0, keepdims=True)
                     scaled.append((t * arep[pl.ds(v, 1), :]).astype(BF16))
-                    weights.append(kst_lo[k] if side == 0 else kst_hi[k])
-                gs[pl.ds(pl.multiple_of(p * SIDE, SIDE), SIDE), :] = dot(
-                    scaled[0], weights[0]
-                ) + dot(scaled[1], weights[1])
-            return carry
-
-        lax.fori_loop(0, 64 // unroll, visit_back, 0)
+            for u, (p, ks) in enumerate(zip(pairs, which)):
+                gs[pl.ds(pl.multiple_of(p * PITCH, 8), SIDE), :] = dot(
+                    scaled[2 * u], kst_lo[ks[0]]
+                ) + dot(scaled[2 * u + 1], kst_hi[ks[1]])
+            return carry
+
+        lax.fori_loop(0, 64 // PAIRS, visit_back, 0)
 
         for half in range(2):
             def grad_body(j, carry, half=half):
                 pair = half * 16 + j
                 mask = lane_lo(64)
-                e = gs[pl.ds(2 * pair, 64, stride=SIDE), :]
-                o = gs[pl.ds(2 * pair + 1, 64, stride=SIDE), :]
+                e = gs[pl.ds(2 * pair, 64, stride=PITCH), :]
+                o = gs[pl.ds(2 * pair + 1, 64, stride=PITCH), :]
                 cols = pl.ds(pl.multiple_of(j * 128, 128), 128)
                 gflat[it, half, 0:64, cols] = jnp.where(mask, e, swap(o)).astype(BF16)
                 gflat[it, half, 64:128, cols] = jnp.where(mask, swap(e), o).astype(BF16)
                 return carry
 
-            lax.fori_loop(0, 16, grad_body, 0)
+            tiled(16, ROWS, grad_body)
         for d in range(4):
             part_copy(it, d, other).start()
         select = jnp.where(
@@ -520,7 +554,7 @@
                 out_m[:, cols] = fresh
             return carry
 
-        lax.fori_loop(0, HALF // 128, update, 0)
+        tiled(16, ROWS, update)
         if it == 0:
             send_visitors(1)
             mine_copy(b).start()
@@ -584,19 +618,19 @@
         pltpu.VMEM((SRC, HALF), F32),
         pltpu.VMEM((2, SRC, HALF), BF16),
         pltpu.VMEM((2, 2, SRC, HALF), BF16),
-        pltpu.VMEM((64 * SIDE, 128), F32),
-        pltpu.VMEM((SLOTS * SIDE, 128), F32),
-        pltpu.VMEM((SLOTS * SIDE, 128), F32),
-        pltpu.VMEM((SLOTS * SIDE, 128), F32),
-        pltpu.VMEM((SLOTS * SIDE, 128), F32),
+        pltpu.VMEM((64 * PITCH, 128), F32),
+        pltpu.VMEM((SLOTS * PITCH, 128), F32),
+        pltpu.VMEM((SLOTS * PITCH, 128), F32),
+        pltpu.VMEM((SLOTS * PITCH, 128), F32),
+        pltpu.VMEM((SLOTS * PITCH, 128), F32),
         pltpu.VMEM((SRC, SIDE, 256), BF16),
         pltpu.VMEM((130, SIDE, 256), F32),
         pltpu.VMEM((SLOTS, SIDE, 256), F32),
         pltpu.VMEM((SLOTS, 256, 256), BF16),
-        pltpu.VMEM((SLOTS * SIDE, 128), F32),
-        pltpu.VMEM((SLOTS * SIDE, 128), F32),
+        pltpu.VMEM((SLOTS * PITCH, 128), F32),
+        pltpu.VMEM((SLOTS * PITCH, 128), F32),
         pltpu.VMEM((2, SRC, HALF), BF16),
-        pltpu.VMEM((64 * SIDE, 128), F32),
+        pltpu.VMEM((64 * PITCH, 128), F32),
         pltpu.VMEM((2, 2, SRC, HALF), BF16),
         pltpu.VMEM((2, SRC, HALF), BF16),
         pltpu.VMEM((2, SRC, HALF), BF16),

time: 183 us -> 105 us (0.57)
  Pallas kernels: 174 us -> 96.2 us
    pallas_call x1, Pallas kernels: 174 us -> 96.2 us  [shards(): pl.pallas_call(functools.partial(deblend, n_ra, n_dec), out_shape=(jax.Sh...]
where the time goes in v1:
time: 105 us
  Pallas kernels  96.2 us (92%)
  local copies, waits for them, and re-layouts  7.26 us (7%)
    pallas_call x1, Pallas kernels, shards(): pl.pallas_call(functools.partial(deblend, n_ra, n_dec), out_shape=(jax.Sh...  96.2 us
    unnamed x12, local copies, waits for them, and re-layouts  6.06 us

profile of v1, /device:TPU:1, one launch (start us, length us, event | category | flops | bytes accessed | tf_op | source)
XLA Modules:
  0.0 104.8 jit_solution(17735864877542785399)
XLA Ops:
  0.6 0.0 copy-start.3
  0.6 0.7 copy-done.3
  1.3 0.0 copy-start.1
  1.3 0.6 copy.15
  1.9 0.1 copy-done.1
  2.0 0.6 copy.14
  2.6 0.9 slice_reduce_fusion.1
  3.5 0.0 copy-start
  3.5 0.1 squeeze.35
  3.6 0.1 squeeze.36
  3.7 0.6 copy-done
  4.3 0.1 reshape.11
  4.4 0.7 maximum_maximum_fusion.psf
  5.1 96.2 %deblend.1 = (f32[128,2048]{1,0:T(8,128)}, f32[3,128]{1,0:T(4,128)}) custom-call(bf16[128,4096]{1,0:T(8,128)(2,1)} %bitcast.18, f32[3,128]{1,0:T(4,128)} %bitcast.22, s32[5,128]{1,0:T(8,128)} %bitcast.21, f32[1,128]{1,0:T(1,128)} %bitcast.24, f32[1,128]{1,0:T(1,128)} %bitcast.25, bf16[96,128]{1,0:T(8,128)(2,1)} %maximum_maximum_fusion.psf, ...), custom_call_target="tpu_custom_call" | custom-call | tf_op jit(solution)/shard_map/deblend/pallas_call | solution.py:650
  101.3 0.0 copy-start.2
  101.3 0.7 copy-done.2
  102.0 0.6 copy.9
  102.5 2.3 %copy.17 = f32[1,1,128,2048]{3,2,1,0:T(8,128)} copy(f32[1,1,128,2048]{3,2,1,0:T(8,128)} %bitcast.19) | data formatting | bytes 2097152
  (1 shorter events, 0.0 us)
Async XLA Ops:
  0.6 0.7 copy-start.3
  1.3 0.7 copy-start.1
  3.5 0.8 copy-start
  101.3 0.7 copy-start.2

commit v2 on v1

--- a/solution.py
+++ b/solution.py
@@ -91,17 +91,17 @@
 
 
 def deblend(
-    n_ra, n_dec,
-    morph, sed, lists, mstep, sstep, psf, obs,
+    n_ra, n_dec, n_x,
+    morph, sed, lists, mstep, sstep, psf_in, obs_in,
     out_m, out_a,
-    kp, k3, kt3, kst_lo, kst_hi,
+    psf_f, psf, obs, kp, k3, kt3, kst_lo, kst_hi,
     lists8, lists_in, amps, amps_in, amp_now,
     pick_out, pick_back, home_amp, home_back, step_col, entries, table,
     mq, mf, vout, vin, xs, s_lo, s_hi, o_lo, o_hi, zs, pfx, model, resid,
     b_lo, b_hi, bflat, gs, gflat, gsum, gin, gret, hown, hsend, hin,
     arep, ga_rows, ga_send, ga_ret, ga_home,
     psf_send, psf_recv, list_sem, amp_sem, vis_sem, fwd_sem, mine_sem, home_sem,
-    part_sem, back_sem, gain_sem, table_sem,
+    part_sem, back_sem, gain_sem, table_sem, load_sem,
 ):
     r = lax.axis_index("ra")
     c = lax.axis_index("dec")
@@ -112,7 +112,11 @@
     target = [(right, c, b), (left, c, b), (r, up, b), (r, down, b)]
     origin = [(left, c, b), (right, c, b), (r, down, b), (r, up, b)]
     sibling = (r, c, other)
-    nk = min(SLOTS, n_ra)
+    n_z = n_ra // n_x
+    x, z = r // n_z, lax.rem(r, n_z)
+    kind = lax.rem(c, 2)
+    kind_k = kind * n_z
+    partner = (r, c + 1 - 2 * kind, b)
 
     def send(src, dst, sems, index, device):
         return pltpu.make_async_remote_copy(
@@ -121,23 +125,45 @@
             device_id=device, device_id_type=MESH,
         )
 
+    def x_peer(step):
+        return (lax.rem(x + step, n_x) * n_z + z, c, b)
+
+    def z_peer(step):
+        return (x * n_z + lax.rem(z + step, n_z), c, b)
+
     barrier = pltpu.get_barrier_semaphore()
-
-    def greet(step, carry):
-        pl.semaphore_signal(
-            barrier, inc=1, device_id=(lax.rem(r + step, n_ra), c, b), device_id_type=MESH
-        )
-        return carry
-
-    lax.fori_loop(1, n_ra, greet, 0)
-    for device in target[2:] + [sibling]:
+    for device in (
+        target
+        + [sibling]
+        + [x_peer(step) for step in range(1, n_x)]
+        + [z_peer(step) for step in range(1, n_z)]
+    ):
         pl.semaphore_signal(barrier, inc=1, device_id=device, device_id_type=MESH)
+    loads = [
+        pltpu.make_async_copy(morph.at[:, pl.ds(HALF * half, HALF)], mq.at[0, half], load_sem.at[half])
+        for half in range(2)
+    ] + [pltpu.make_async_copy(obs_in, obs, load_sem.at[2])]
+    for load in loads:
+        load.start()
     lists8[...] = jnp.full((8, SRC), SLOTS, I32)
-    lists8[0:5, :] = lists[...]
+    for d in range(5):
+        lists8[d : d + 1, :] = lists[d]
     amp_now[...] = jnp.zeros((8, SRC), F32)
-    amp_now[0:3, :] = sed[...]
+    for band in range(3):
+        amp_now[band : band + 1, :] = sed[band]
     amps[0] = amp_now[...].astype(BF16).astype(F32)
-    pl.semaphore_wait(barrier, n_ra - 1 + 3)
+    own = psf_in[...].astype(F32)
+    for j in range(32):
+        x0, x1 = own[0:1, 128 * j : 128 * j + 128], own[1:2, 128 * j : 128 * j + 128]
+        psf_f[2 * j : 2 * j + 1, :] = jnp.where(lane_lo(1), x0, swap(x1))
+        psf_f[2 * j + 1 : 2 * j + 2, :] = jnp.where(lane_lo(1), swap(x0), x1)
+    for j in range(16):
+        x0 = own[2:3, 128 * j : 128 * j + 128]
+        x1 = own[2:3, HALF + 128 * j : HALF + 128 * j + 128]
+        psf_f[64 + 2 * j : 65 + 2 * j, :] = jnp.where(lane_lo(1), x0, swap(x1))
+        psf_f[65 + 2 * j : 66 + 2 * j, :] = jnp.where(lane_lo(1), swap(x0), x1)
+    psf[...] = psf_f[...].astype(BF16)
+    pl.semaphore_wait(barrier, 5 + n_x - 1 + n_z - 1)
 
     list_copies = [
         send(lists8, lists_in.at[d], list_sem, (d,), target[d]) for d in range(4)
@@ -145,20 +171,52 @@
     for copy in list_copies:
         copy.start()
 
-    def psf_copy(step):
+    def psf_copy(k, index, device):
         return pltpu.make_async_remote_copy(
-            src_ref=psf, dst_ref=kp.at[lax.rem(r, SLOTS)],
-            send_sem=psf_send.at[step], recv_sem=psf_recv.at[lax.rem(r, SLOTS)],
-            device_id=(lax.rem(r + step, n_ra), c, b), device_id_type=MESH,
-        )
-
-    def spread_psf():
-        def body(step, carry):
-            psf_copy(step).start()
-            return carry
-
-        lax.fori_loop(1, n_ra, body, 0)
-        kp[lax.rem(r, SLOTS)] = psf[...]
+            src_ref=kp.at[k], dst_ref=kp.at[k],
+            send_sem=psf_send.at[index], recv_sem=psf_recv.at[k],
+            device_id=device, device_id_type=MESH,
+        )
+
+    def x_copy(step):
+        return psf_copy(kind_k + z, step - 1, x_peer(step))
+
+    def z_copy(step):
+        return psf_copy(kind_k + z, n_x + step - 1, z_peer(step))
+
+    def z_arrival(step):
+        return psf_copy(kind_k + lax.rem(z + step, n_z), 0, z_peer(step))
+
+    def y_copy(step):
+        return psf_copy(kind_k + lax.rem(z + step, n_z), n_x + n_z + step, partner)
+
+    def y_arrival(step):
+        return psf_copy(n_z - kind_k + lax.rem(z + step, n_z), 0, partner)
+
+    @pl.when(x == kind)
+    def _():
+        kp[kind_k + z] = psf[...]
+        for step in range(1, n_x):
+            x_copy(step).start()
+
+    def psf_along_z():
+        @pl.when(x != kind)
+        def _():
+            psf_copy(kind_k + z, 0, sibling).wait_recv()
+
+        for step in range(1, n_z):
+            z_copy(step).start()
+        y_copy(0).start()
+
+    def psf_along_y():
+        for near in range(1, n_z // 2 + 1):
+            for step in sorted({near, n_z - near}):
+                z_arrival(step).wait_recv()
+                y_copy(step).start()
+
+    def psf_here():
+        for step in range(n_z):
+            y_arrival(step).wait_recv()
 
     def amp_copy(it, d):
         return send(amps.at[it], amps_in.at[it, d], amp_sem, (it, d), target[d])
@@ -199,9 +257,8 @@
     pick_out[...] = pick
     pick_back[...] = pick.T.astype(BF16)
 
-    mq[0, 0] = morph[:, 0:HALF]
-    mq[0, 1] = morph[:, HALF : 2 * HALF]
-    mf[...] = mq[0, b].astype(F32)
+    for load in loads:
+        load.wait()
 
     def send_visitors(it):
         def body(j, carry):
@@ -215,12 +272,10 @@
 
     send_visitors(0)
 
-    @pl.when(r < SLOTS)
-    def _():
-        spread_psf()
-
-    if nk < SLOTS:
-        kp[nk:SLOTS] = jnp.zeros((SLOTS - nk, 96, 128), BF16)
+    psf_along_z()
+    mf[...] = mq[0, b].astype(F32)
+    if 2 * n_z < SLOTS:
+        kp[2 * n_z : SLOTS] = jnp.zeros((SLOTS - 2 * n_z, 96, 128), BF16)
 
     step_col[...] = turned(mstep[...])
     slot0 = lists8[0:1, :]
@@ -311,68 +366,68 @@
 
             tiled(16, ROWS, sum_body)
 
+        def home_forward():
+            if it == 0:
+                psf_here()
+
+                def unpack_body(q, carry):
+                    unpack(q)
+                    return carry
+
+                tiled(SLOTS, 4, unpack_body)
+
+            def home_model(step, carry):
+                slots = [step * HOME + u for u in range(HOME)]
+                z = []
+                for q in slots:
+                    rows = pl.ds(pl.multiple_of(q * PITCH, 8), SIDE)
+                    s = jnp.concatenate([s_lo[rows, :], s_hi[rows, :]], axis=1).astype(BF16)
+                    kt = kt3[q]
+                    z.append(dot(s, block_diag(kt[:, 0:128], kt[:, 128:256])).astype(BF16))
+                for q, zq in zip(slots, z):
+                    model[q] = dot(k3[q], block_diag(zq[:, 0:128], zq[:, 128:256]))
+                return carry
+
+            lax.fori_loop(0, SLOTS // HOME, home_model, 0)
+
+        def visitors_in():
+            for d in range(4):
+                amp_copy(it, d).wait_recv()
+                picked = entries[pl.ds(CAP * d, CAP), :].astype(F32)
+                cols = [
+                    jnp.sum(picked * amps_in[it, d, band : band + 1, :], axis=1, keepdims=True)
+                    for band in range(3)
+                ]
+                mask = lane_lo(CAP)
+                rows = pl.ds(CAP * d, CAP)
+                arep[rows, 0:128] = jnp.where(mask, cols[0], cols[1])
+                arep[rows, 128:256] = jnp.where(mask, cols[2], 0.0)
+
+            for d in range(4):
+                vis_copy(it, d).wait_recv()
+                fwd_copy(it, d, b).start()
+            for d in range(4):
+                fwd_copy(it, d, other).wait_recv()
+            for half in range(2):
+                def stamp_body(j, carry, half=half):
+                    cols = pl.ds(pl.multiple_of(j * 128, 128), 128)
+                    mask = lane_lo(64)
+                    xa = vin[it, half, 0:64, cols].astype(F32)
+                    xb = vin[it, half, 64:128, cols].astype(F32)
+                    pair = half * 16 + j
+                    xs[pl.ds(2 * pair, 64, stride=PITCH), :] = jnp.where(mask, xa, swap(xb))
+                    xs[pl.ds(2 * pair + 1, 64, stride=PITCH), :] = jnp.where(mask, swap(xa), xb)
+                    return carry
+
+                tiled(16, ROWS, stamp_body)
+
         if it == 0:
-            def ready(q, carry):
-                @pl.when(jnp.logical_and(q != r, q < nk))
-                def _():
-                    pltpu.make_async_remote_copy(
-                        src_ref=psf, dst_ref=kp.at[q], send_sem=psf_send.at[0],
-                        recv_sem=psf_recv.at[q], device_id=sibling, device_id_type=MESH,
-                    ).wait_recv()
-
-                return carry
-
-            lax.fori_loop(0, SLOTS, ready, 0)
-
-            def unpack_body(q, carry):
-                unpack(q)
-                return carry
-
-            tiled(SLOTS, 4, unpack_body)
-
-        def home_model(step, carry):
-            slots = [step * HOME + u for u in range(HOME)]
-            z = []
-            for q in slots:
-                rows = pl.ds(pl.multiple_of(q * PITCH, 8), SIDE)
-                s = jnp.concatenate([s_lo[rows, :], s_hi[rows, :]], axis=1).astype(BF16)
-                kt = kt3[q]
-                z.append(dot(s, block_diag(kt[:, 0:128], kt[:, 128:256])).astype(BF16))
-            for q, zq in zip(slots, z):
-                model[q] = dot(k3[q], block_diag(zq[:, 0:128], zq[:, 128:256]))
-            return carry
-
-        lax.fori_loop(0, SLOTS // HOME, home_model, 0)
-
-        for d in range(4):
-            amp_copy(it, d).wait_recv()
-            picked = entries[pl.ds(CAP * d, CAP), :].astype(F32)
-            cols = [
-                jnp.sum(picked * amps_in[it, d, band : band + 1, :], axis=1, keepdims=True)
-                for band in range(3)
-            ]
-            mask = lane_lo(CAP)
-            rows = pl.ds(CAP * d, CAP)
-            arep[rows, 0:128] = jnp.where(mask, cols[0], cols[1])
-            arep[rows, 128:256] = jnp.where(mask, cols[2], 0.0)
-
-        for d in range(4):
-            vis_copy(it, d).wait_recv()
-            fwd_copy(it, d, b).start()
-        for d in range(4):
-            fwd_copy(it, d, other).wait_recv()
-        for half in range(2):
-            def stamp_body(j, carry, half=half):
-                cols = pl.ds(pl.multiple_of(j * 128, 128), 128)
-                mask = lane_lo(64)
-                xa = vin[it, half, 0:64, cols].astype(F32)
-                xb = vin[it, half, 64:128, cols].astype(F32)
-                pair = half * 16 + j
-                xs[pl.ds(2 * pair, 64, stride=PITCH), :] = jnp.where(mask, xa, swap(xb))
-                xs[pl.ds(2 * pair + 1, 64, stride=PITCH), :] = jnp.where(mask, swap(xa), xb)
-                return carry
-
-            tiled(16, ROWS, stamp_body)
+            psf_along_y()
+            visitors_in()
+            home_forward()
+        else:
+            home_forward()
+            visitors_in()
 
         def visit_model(step, carry):
             acc = list(carry)
@@ -399,10 +454,9 @@
         start = jnp.zeros((SIDE, 256), F32)
         lax.fori_loop(0, 64 // PAIRS, visit_model, (start, start))
 
-        def home_back_body(step, carry):
-            slots = [step * HOME + u for u in range(HOME)]
-            diags = []
-            for q in slots:
+        def residual(step, carry):
+            for u in range(HOME // 2):
+                q = step * (HOME // 2) + u
                 total = model[q]
                 for d in range(4):
                     base = (0, 32, 65, 97)[d]
@@ -410,9 +464,77 @@
                 rows = pl.ds(pl.multiple_of(q * PITCH, 8), SIDE)
                 seen = jnp.concatenate([o_lo[rows, :], o_hi[rows, :]], axis=1)
                 res = (total - seen).astype(BF16)
-                diags.append(block_diag(res[:, 0:128], res[:, 128:256]))
-                resid[q] = diags[-1]
-            turns = [dot(kt3[q], diag).astype(BF16) for q, diag in zip(slots, diags)]
+                resid[q] = block_diag(res[:, 0:128], res[:, 128:256])
+            return carry
+
+        lax.fori_loop(0, SLOTS // (HOME // 2), residual, 0)
+
+        def visit_back(step, carry):
+            pairs = [step * PAIRS + u for u in range(PAIRS)]
+            which = [[smem[0, p + 64 * side] for side in range(2)] for p in pairs]
+            scaled = []
+            for p, ks in zip(pairs, which):
+                for side in range(2):
+                    v = p + 64 * side
+                    t = dot(kt3[ks[side]], resid[smem[1, v]])
+                    ga_rows[pl.ds(v, 1), :] = jnp.sum(t * zs[v].astype(F32), axis=0, keepdims=True)
+                    scaled.append((t * arep[pl.ds(v, 1), :]).astype(BF16))
+            for u, (p, ks) in enumerate(zip(pairs, which)):
+                gs[pl.ds(pl.multiple_of(p * PITCH, 8), SIDE), :] = dot(
+                    scaled[2 * u], kst_lo[ks[0]]
+                ) + dot(scaled[2 * u + 1], kst_hi[ks[1]])
+            return carry
+
+        def flatten(first):
+            for half in range(2):
+                def grad_body(j, carry, half=half):
+                    pair = half * 16 + j
+                    mask = lane_lo(32)
+                    e = gs[pl.ds(first * PITCH + 2 * pair, 32, stride=PITCH), :]
+                    o = gs[pl.ds(first * PITCH + 2 * pair + 1, 32, stride=PITCH), :]
+                    cols = pl.ds(pl.multiple_of(j * 128, 128), 128)
+                    gflat[it, half, first : first + 32, cols] = jnp.where(mask, e, swap(o)).astype(BF16)
+                    gflat[it, half, 64 + first : 96 + first, cols] = jnp.where(
+                        mask, swap(e), o
+                    ).astype(BF16)
+                    return carry
+
+                tiled(16, ROWS, grad_body)
+
+        def give_back(d):
+            part_copy(it, d, other).wait_recv()
+            rows = pl.ds(CAP * d, CAP)
+            gsum[it, rows, :] = (
+                gflat[it, b, rows, :].astype(F32) + gin[it, rows, :].astype(F32)
+            ).astype(BF16)
+            back_copy(it, d).start()
+
+        lax.fori_loop(0, 32 // PAIRS, visit_back, 0)
+        flatten(0)
+        for d in (0, 2):
+            part_copy(it, d, other).start()
+        lax.fori_loop(32 // PAIRS, 64 // PAIRS, visit_back, 0)
+        flatten(32)
+        for d in (1, 3):
+            part_copy(it, d, other).start()
+        for d in (0, 2):
+            give_back(d)
+        select = jnp.where(
+            lax.broadcasted_iota(I32, (8, 256), 1) // SIDE
+            == lax.broadcasted_iota(I32, (8, 256), 0),
+            1.0,
+            0.0,
+        )
+        ga_send[it] = lax.dot_general(
+            select, ga_rows[...], (((1,), (1,)), ((), ())),
+            preferred_element_type=F32, precision=lax.Precision.HIGHEST,
+        )
+        for d in range(4):
+            gain_copy(it, d).start()
+
+        def home_back_body(step, carry):
+            slots = [step * HOME + u for u in range(HOME)]
+            turns = [dot(kt3[q], resid[q]).astype(BF16) for q in slots]
             for q, t in zip(slots, turns):
                 rows = pl.ds(pl.multiple_of(q * PITCH, 8), SIDE)
                 kk = k3[q]
@@ -422,6 +544,8 @@
             return carry
 
         lax.fori_loop(0, SLOTS // HOME, home_back_body, 0)
+        for d in (1, 3):
+            give_back(d)
 
         for half in range(2):
             def flat_body(j, carry, half=half):
@@ -471,58 +595,6 @@
             axis=0,
         )
 
-        def visit_back(step, carry):
-            pairs = [step * PAIRS + u for u in range(PAIRS)]
-            which = [[smem[0, p + 64 * side] for side in range(2)] for p in pairs]
-            scaled = []
-            for p, ks in zip(pairs, which):
-                for side in range(2):
-                    v = p + 64 * side
-                    t = dot(kt3[ks[side]], resid[smem[1, v]])
-                    ga_rows[pl.ds(v, 1), :] = jnp.sum(t * zs[v].astype(F32), axis=0, keepdims=True)
-                    scaled.append((t * arep[pl.ds(v, 1), :]).astype(BF16))
-            for u, (p, ks) in enumerate(zip(pairs, which)):
-                gs[pl.ds(pl.multiple_of(p * PITCH, 8), SIDE), :] = dot(
-                    scaled[2 * u], kst_lo[ks[0]]
-                ) + dot(scaled[2 * u + 1], kst_hi[ks[1]])
-            return carry
-
-        lax.fori_loop(0, 64 // PAIRS, visit_back, 0)
-
-        for half in range(2):
-            def grad_body(j, carry, half=half):
-                pair = half * 16 + j
-                mask = lane_lo(64)
-                e = gs[pl.ds(2 * pair, 64, stride=PITCH), :]
-                o = gs[pl.ds(2 * pair + 1, 64, stride=PITCH), :]
-                cols = pl.ds(pl.multiple_of(j * 128, 128), 128)
-                gflat[it, half, 0:64, cols] = jnp.where(mask, e, swap(o)).astype(BF16)
-                gflat[it, half, 64:128, cols] = jnp.where(mask, swap(e), o).astype(BF16)
-                return carry
-
-            tiled(16, ROWS, grad_body)
-        for d in range(4):
-            part_copy(it, d, other).start()
-        select = jnp.where(
-            lax.broadcasted_iota(I32, (8, 256), 1) // SIDE
-            == lax.broadcasted_iota(I32, (8, 256), 0),
-            1.0,
-            0.0,
-        )
-        ga_send[it] = lax.dot_general(
-            select, ga_rows[...], (((1,), (1,)), ((), ())),
-            preferred_element_type=F32, precision=lax.Precision.HIGHEST,
-        )
-        for d in range(4):
-            gain_copy(it, d).start()
-        for d in range(4):
-            part_copy(it, d, other).wait_recv()
-            rows = pl.ds(CAP * d, CAP)
-            gsum[it, rows, :] = (
-                gflat[it, b, rows, :].astype(F32) + gin[it, rows, :].astype(F32)
-            ).astype(BF16)
-            back_copy(it, d).start()
-
         lane = lax.broadcasted_iota(I32, (8, SRC), 1) // CAP
         returned = jnp.zeros((8, SRC), F32)
         for d in range(4):
@@ -531,13 +603,15 @@
         gain = ga_home[...] + jnp.dot(
             returned, pick_out[...], preferred_element_type=F32, precision=lax.Precision.HIGHEST
         )
-        amp_now[...] = jnp.maximum(amp_now[...] - sstep[...] * gain, 0.0)
+        amp_now[...] = amp_now[...] - sstep[...] * gain
         if it == 0:
+            amp_now[...] = jnp.maximum(amp_now[...], 0.0)
             amps[1] = amp_now[...].astype(BF16).astype(F32)
             for d in range(4):
                 amp_copy(1, d).start()
         else:
-            out_a[...] = amp_now[0:3, :]
+            for band in range(3):
+                out_a[band] = amp_now[band : band + 1, :]
         home_copy(it).wait_recv()
         for d in range(4):
             back_copy(it, d).wait_recv()
@@ -546,8 +620,9 @@
             cols = pl.ds(pl.multiple_of(j * 128, 128), 128)
             grad = hown[:, cols] + hin[it, :, cols].astype(F32)
             grad = grad + dot(pick_back[...], gret[it, :, cols])
-            fresh = jnp.maximum(mf[:, cols] - step_col[...] * grad, 0.0)
+            fresh = mf[:, cols] - step_col[...] * grad
             if it == 0:
+                fresh = jnp.maximum(fresh, 0.0)
                 mf[:, cols] = fresh
                 mq[1, b, :, cols] = fresh.astype(BF16)
             else:
@@ -575,28 +650,27 @@
             back_copy(it, d).wait_send()
             gain_copy(it, d).wait_send()
 
-    @pl.when(r < SLOTS)
+    @pl.when(x == kind)
     def _():
-        def body(step, carry):
-            psf_copy(step).wait_send()
-            return carry
-
-        lax.fori_loop(1, n_ra, body, 0)
+        for step in range(1, n_x):
+            x_copy(step).wait_send()
+
+    for step in range(1, n_z):
+        z_copy(step).wait_send()
+    for step in range(n_z):
+        y_copy(step).wait_send()
 
 
 def shards(morphology, sed_amps, slot_lists, morph_step, sed_step, psf_kernels, observed):
     n_ra, n_dec = lax.axis_size("ra"), lax.axis_size("dec")
-    kernels = psf_kernels.reshape(3, SIDE, SIDE)
-    packed = jnp.concatenate(
-        [
-            jnp.concatenate([kernels[0], kernels[1]], axis=1),
-            jnp.concatenate([kernels[2, :32], kernels[2, 32:]], axis=1),
-        ],
-        axis=0,
-    )
+    n_x = 4 if n_ra == 32 else 2
     vmem = pl.BlockSpec(memory_space=pltpu.VMEM)
+    hbm = pl.BlockSpec(memory_space=pl.ANY)
     dma = pltpu.SemaphoreType.DMA
     scratch = [
+        pltpu.VMEM((96, 128), F32),
+        pltpu.VMEM((96, 128), BF16),
+        pltpu.VMEM((3, SLOTS, 2 * HALF), BF16),
         pltpu.VMEM((SLOTS, 96, 128), BF16),
         pltpu.VMEM((SLOTS, SIDE, 256), BF16),
         pltpu.VMEM((SLOTS, SIDE, 256), BF16),
@@ -643,17 +717,17 @@
         pltpu.VMEM((2, 8, SRC), F32),
         pltpu.VMEM((2, 4, 8, SRC), F32),
         pltpu.VMEM((8, SRC), F32),
-        dma((n_ra,)), dma((SLOTS,)),
+        dma((n_x + 2 * (n_ra // n_x),)), dma((SLOTS,)),
         dma((2, 4)), dma((2, 2, 4)), dma((2, 2, 4)), dma((2, 2, 4)), dma((2, 1)), dma((2, 2)),
-        dma((2, 2, 4)), dma((2, 2, 4)), dma((2, 2, 4)), dma,
+        dma((2, 2, 4)), dma((2, 2, 4)), dma((2, 2, 4)), dma, dma((3,)),
     ]
     out_m, out_a = pl.pallas_call(
-        functools.partial(deblend, n_ra, n_dec),
+        functools.partial(deblend, n_ra, n_dec, n_x),
         out_shape=(
             jax.ShapeDtypeStruct((SRC, HALF), F32),
-            jax.ShapeDtypeStruct((3, SRC), F32),
+            jax.ShapeDtypeStruct((3, 1, SRC), F32),
         ),
-        in_specs=[vmem] * 7,
+        in_specs=[hbm] + [vmem] * 5 + [hbm],
         out_specs=(vmem, vmem),
         scratch_shapes=scratch,
         compiler_params=pltpu.CompilerParams(
@@ -661,10 +735,11 @@
         ),
         name="deblend",
     )(
-        morphology[0, 0], sed_amps[0, 0], slot_lists[0, 0], morph_step[0], sed_step[0],
-        packed, observed[0, 0],
+        morphology[0, 0], sed_amps.reshape(3, 1, SRC), slot_lists.reshape(5, 1, SRC),
+        morph_step[0], sed_step[0], psf_kernels.reshape(3, 2 * HALF), observed[0, 0],
     )
-    return out_m[None, None], out_a[None, None]
+    out_m, out_a = jnp.maximum(out_m, 0.0), jnp.maximum(out_a, 0.0)
+    return out_m[None, None], out_a.reshape(1, 1, 3, SRC)
 
 
 def solution(mesh):

time: 105 us -> 83.6 us (0.80)
  Pallas kernels: 96.2 us -> 79.9 us
  local copies, waits for them, and re-layouts: 7.26 us -> 0.01 us
  other arithmetic: 0.69 us -> 2.86 us
    pallas_call x1, Pallas kernels: 96.2 us -> 79.9 us  [shards(): pl.pallas_call(functools.partial(deblend, n_ra, n_dec, n_x), out_shape=(j...]
    unnamed x12 -> x2, local copies, waits for them, and re-layouts: 6.06 us -> 0.01 us
    broadcast_in_dim x0 -> x1, other arithmetic: none -> 2.29 us  [shards(): return (out_m[None, None], out_a.reshape(1, 1, 3, SRC))]
where the time goes in v2:
time: 83.6 us; the launch traced here: 83.4 us
  Pallas kernels  79.9 us (96%)
  other arithmetic  2.86 us (3%)
    pallas_call x1, Pallas kernels, shards(): pl.pallas_call(functools.partial(deblend, n_ra, n_dec, n_x), out_shape=(j...  79.9 us
    broadcast_in_dim x1, other arithmetic, shards(): return (out_m[None, None], out_a.reshape(1, 1, 3, SRC))  2.29 us

profile of v2, /device:TPU:1, one launch (start us, length us, event | category | flops | bytes accessed | tf_op | source)
XLA Modules:
  0.0 83.4 jit_solution(6623150374229522469)
XLA Ops:
  0.6 79.9 %deblend.1 = (f32[128,2048]{1,0:T(8,128)}, f32[3,1,128]{2,1,0:T(1,128)}) custom-call(bf16[128,4096]{1,0:T(8,128)(2,1)} %bitcast.13, f32[3,1,128]{2,1,0:T(1,128)} %bitcast.17, s32[5,1,128]{2,1,0:T(1,128)} %bitcast.16, f32[1,128]{1,0:T(1,128)} %bitcast.18, f32[1,128]{1,0:T(1,128)} %bitcast.19, bf16[3,4096]{1,0:T(4,128)(2,1)} %bitcast.15, ...), custom_call_target="tpu_custom_call" | custom-call | tf_op jit(solution)/shard_map/deblend/pallas_call | solution.py:724
  80.5 0.0 copy-start
  80.5 2.3 %maximum_bitcast_fusion = f32[1,1,128,2048]{3,2,1,0:T(8,128)} fusion(f32[128,2048]{1,0:T(8,128)} %get-tuple-element.4), kind=kLoop, calls=%fused_computation | loop fusion | flops 262144 | bytes 2097152 | tf_op jit(solution)/shard_map/broadcast_in_dim | solution.py:742
  82.8 0.0 copy-done
  82.8 0.6 maximum_bitcast_fusion.1
Async XLA Ops:
  80.5 2.3 %copy-start = (f32[3,1,128]{2,1,0:T(1,128)S(1)}, f32[3,1,128]{2,1,0:T(1,128)}, u32[]{:S(2)}) copy-start(f32[3,1,128]{2,1,0:T(1,128)} %get-tuple-element.5) | copy-start | bytes 4612

commit v3 on v2

--- a/solution.py
+++ b/solution.py
@@ -13,10 +13,12 @@
 CAP = 32
 SRC = 128
 HALF = 2048
+PART = CAP // 2
+BASE = (0, 33, 66, 99)
 PITCH = 72
 ROWS = 8
 HOME = 8
-PAIRS = 8
+QUADS = 8
 MESH = pl.DeviceIdType.MESH
 F32 = jnp.float32
 BF16 = jnp.bfloat16
@@ -96,7 +98,7 @@
     out_m, out_a,
     psf_f, psf, obs, kp, k3, kt3, kst_lo, kst_hi,
     lists8, lists_in, amps, amps_in, amp_now,
-    pick_out, pick_back, home_amp, home_back, step_col, entries, table,
+    pick_out, pick_back, home_amp, home_back, step_col, entries, table, smem,
     mq, mf, vout, vin, xs, s_lo, s_hi, o_lo, o_hi, zs, pfx, model, resid,
     b_lo, b_hi, bflat, gs, gflat, gsum, gin, gret, hown, hsend, hin,
     arep, ga_rows, ga_send, ga_ret, ga_home,
@@ -221,13 +223,13 @@
     def amp_copy(it, d):
         return send(amps.at[it], amps_in.at[it, d], amp_sem, (it, d), target[d])
 
-    def vis_copy(it, d):
-        rows = pl.ds(CAP * d, CAP)
-        return send(vout.at[it, rows], vin.at[it, b, rows], vis_sem, (it, d), target[d])
-
-    def fwd_copy(it, d, half):
-        rows = pl.ds(CAP * d, CAP)
-        return send(vin.at[it, half, rows], vin.at[it, half, rows], fwd_sem, (it, d), sibling)
+    def vis_copy(it, d, part):
+        rows = pl.ds(CAP * d + PART * part, PART)
+        return send(vout.at[it, rows], vin.at[it, b, rows], vis_sem, (it, d, part), target[d])
+
+    def fwd_copy(it, d, part, half):
+        rows = pl.ds(CAP * d + PART * part, PART)
+        return send(vin.at[it, half, rows], vin.at[it, half, rows], fwd_sem, (it, d, part), sibling)
 
     def mine_copy(half):
         return send(mq.at[1, half], mq.at[1, half], mine_sem, (0,), sibling)
@@ -235,13 +237,13 @@
     def home_copy(it):
         return send(hsend.at[it], hin.at[it], home_sem, (it,), sibling)
 
-    def part_copy(it, d, half):
-        rows = pl.ds(CAP * d, CAP)
-        return send(gflat.at[it, half, rows], gin.at[it, rows], part_sem, (it, d), sibling)
-
-    def back_copy(it, d):
-        rows = pl.ds(CAP * d, CAP)
-        return send(gsum.at[it, rows], gret.at[it, rows], back_sem, (it, d), origin[d])
+    def part_copy(it, d, part, half):
+        rows = pl.ds(CAP * d + PART * part, PART)
+        return send(gflat.at[it, half, rows], gin.at[it, rows], part_sem, (it, d, part), sibling)
+
+    def back_copy(it, d, part):
+        rows = pl.ds(CAP * d + PART * part, PART)
+        return send(gsum.at[it, rows], gret.at[it, rows], back_sem, (it, d, part), origin[d])
 
     def gain_copy(it, d):
         return send(ga_send.at[it], ga_ret.at[it, d], gain_sem, (it, d), origin[d])
@@ -266,9 +268,10 @@
             vout[it, :, cols] = dot(pick_out[...].astype(BF16), mq[it, b, :, cols]).astype(BF16)
             return carry
 
-        lax.fori_loop(0, HALF // 256, body, 0)
-        for d in range(4):
-            vis_copy(it, d).start()
+        tiled(8, 8, body)
+        for part in range(2):
+            for d in range(4):
+                vis_copy(it, d, part).start()
 
     send_visitors(0)
 
@@ -282,7 +285,8 @@
     is_slot = jnp.where(slot0 == lax.broadcasted_iota(I32, (SLOTS, SRC), 0), 1.0, 0.0)
     bflat[...] = jnp.zeros(bflat.shape, BF16)
     pfx[0] = jnp.zeros((SIDE, 256), F32)
-    pfx[65] = jnp.zeros((SIDE, 256), F32)
+    for d in range(1, 4):
+        pfx[BASE[d]] = jnp.zeros((SIDE, 256), F32)
 
     for half in range(2):
         def obs_body(j, carry, half=half):
@@ -313,15 +317,9 @@
         table[1:2, :] = jnp.minimum(
             jnp.sum(jnp.concatenate(second, axis=0).T, axis=0, keepdims=True), SLOTS - 1
         )
-
-    take_lists()
-
-    def with_table(smem):
         copy = pltpu.make_async_copy(table, smem, table_sem)
         copy.start()
         copy.wait()
-        for it in range(ITERS):
-            one_iteration(it, smem)
 
     def home_weights(it):
         rows = [is_slot * amps[it, band : band + 1, :] for band in range(3)]
@@ -354,7 +352,7 @@
         kst_hi[k, 128:192, :] = swap(p2).astype(BF16)
         kst_hi[k, 192:256, :] = zero
 
-    def one_iteration(it, smem):
+    def one_iteration(it):
         home_weights(it)
 
         for half in range(2):
@@ -366,7 +364,7 @@
 
             tiled(16, ROWS, sum_body)
 
-        def home_forward():
+        def home_convolved():
             if it == 0:
                 psf_here()
 
@@ -390,7 +388,7 @@
 
             lax.fori_loop(0, SLOTS // HOME, home_model, 0)
 
-        def visitors_in():
+        def visitor_amps():
             for d in range(4):
                 amp_copy(it, d).wait_recv()
                 picked = entries[pl.ds(CAP * d, CAP), :].astype(F32)
@@ -403,63 +401,81 @@
                 arep[rows, 0:128] = jnp.where(mask, cols[0], cols[1])
                 arep[rows, 128:256] = jnp.where(mask, cols[2], 0.0)
 
+        def pass_on(part):
             for d in range(4):
-                vis_copy(it, d).wait_recv()
-                fwd_copy(it, d, b).start()
+                vis_copy(it, d, part).wait_recv()
+                fwd_copy(it, d, part, b).start()
+
+        def visitor_stamps(part):
             for d in range(4):
-                fwd_copy(it, d, other).wait_recv()
+                fwd_copy(it, d, part, other).wait_recv()
             for half in range(2):
                 def stamp_body(j, carry, half=half):
                     cols = pl.ds(pl.multiple_of(j * 128, 128), 128)
-                    mask = lane_lo(64)
-                    xa = vin[it, half, 0:64, cols].astype(F32)
-                    xb = vin[it, half, 64:128, cols].astype(F32)
+                    mask = lane_lo(PART)
                     pair = half * 16 + j
-                    xs[pl.ds(2 * pair, 64, stride=PITCH), :] = jnp.where(mask, xa, swap(xb))
-                    xs[pl.ds(2 * pair + 1, 64, stride=PITCH), :] = jnp.where(mask, swap(xa), xb)
+                    for first in (PART * part, CAP + PART * part):
+                        xa = vin[it, half, first : first + PART, cols].astype(F32)
+                        xb = vin[it, half, 64 + first : 64 + first + PART, cols].astype(F32)
+                        row = first * PITCH + 2 * pair
+                        xs[pl.ds(row, PART, stride=PITCH), :] = jnp.where(mask, xa, swap(xb))
+                        xs[pl.ds(row + 1, PART, stride=PITCH), :] = jnp.where(mask, swap(xa), xb)
                     return carry
 
                 tiled(16, ROWS, stamp_body)
 
+        def visit_model(step, carry):
+            blank = jnp.zeros((SIDE, 256), BF16)
+            acc = [pfx[BASE[d] + step * QUADS] for d in range(4)]
+            z = []
+            for u in range(QUADS):
+                p = step * QUADS + u
+                for side in range(2):
+                    row = pl.multiple_of((p + CAP * side) * PITCH, 8)
+                    x = xs[pl.ds(row, SIDE), :].astype(BF16)
+                    for d in (side, side + 2):
+                        k = smem[0, CAP * d + p]
+                        kt = kt3[k]
+                        weights = jnp.concatenate([kt, blank] if d < 2 else [blank, kt], axis=0)
+                        z.append((d, p, k, dot(x, weights).astype(BF16)))
+            for d, p, k, zv in z:
+                v = CAP * d + p
+                zs[v] = zv
+                conv = dot(k3[k], block_diag(zv[:, 0:128], zv[:, 128:256]))
+                acc[d] = acc[d] + conv * arep[pl.ds(v, 1), :]
+                pfx[BASE[d] + p + 1] = acc[d]
+            return carry
+
+        def visitors_modelled(part):
+            steps = PART // QUADS
+            lax.fori_loop(part * steps, (part + 1) * steps, visit_model, 0)
+
         if it == 0:
+            take_lists()
             psf_along_y()
-            visitors_in()
-            home_forward()
+            visitor_amps()
+            pass_on(0)
+            pass_on(1)
+            visitor_stamps(0)
+            visitor_stamps(1)
+            home_convolved()
         else:
-            home_forward()
-            visitors_in()
-
-        def visit_model(step, carry):
-            acc = list(carry)
-            blank = jnp.zeros((SIDE, 256), BF16)
-            pairs = [step * PAIRS + u for u in range(PAIRS)]
-            which = [[smem[0, p + 64 * side] for side in range(2)] for p in pairs]
-            z = []
-            for p, ks in zip(pairs, which):
-                x = xs[pl.ds(pl.multiple_of(p * PITCH, 8), SIDE), :].astype(BF16)
-                for side in range(2):
-                    kt = kt3[ks[side]]
-                    weights = jnp.concatenate([kt, blank] if side == 0 else [blank, kt], axis=0)
-                    z.append(dot(x, weights).astype(BF16))
-            for u, (p, ks) in enumerate(zip(pairs, which)):
-                for side in range(2):
-                    v = p + 64 * side
-                    zv = z[2 * u + side]
-                    zs[v] = zv
-                    conv = dot(k3[ks[side]], block_diag(zv[:, 0:128], zv[:, 128:256]))
-                    acc[side] = acc[side] + conv * arep[pl.ds(v, 1), :]
-                    pfx[65 * side + p + 1] = acc[side]
-            return tuple(acc)
-
-        start = jnp.zeros((SIDE, 256), F32)
-        lax.fori_loop(0, 64 // PAIRS, visit_model, (start, start))
+            home_convolved()
+            visitor_amps()
+            pass_on(0)
+            visitor_stamps(0)
+            pass_on(1)
+        visitors_modelled(0)
+        if it > 0:
+            visitor_stamps(1)
+        visitors_modelled(1)
 
         def residual(step, carry):
             for u in range(HOME // 2):
                 q = step * (HOME // 2) + u
                 total = model[q]
                 for d in range(4):
-                    base = (0, 32, 65, 97)[d]
+                    base = BASE[d]
                     total = total + (pfx[base + smem[d + 2, q + 1]] - pfx[base + smem[d + 2, q]])
                 rows = pl.ds(pl.multiple_of(q * PITCH, 8), SIDE)
                 seen = jnp.concatenate([o_lo[rows, :], o_hi[rows, :]], axis=1)
@@ -470,55 +486,61 @@
         lax.fori_loop(0, SLOTS // (HOME // 2), residual, 0)
 
         def visit_back(step, carry):
-            pairs = [step * PAIRS + u for u in range(PAIRS)]
-            which = [[smem[0, p + 64 * side] for side in range(2)] for p in pairs]
             scaled = []
-            for p, ks in zip(pairs, which):
+            for u in range(QUADS):
+                p = step * QUADS + u
+                for d in (0, 2, 1, 3):
+                    v = CAP * d + p
+                    k = smem[0, v]
+                    t = dot(kt3[k], resid[smem[1, v]])
+                    ga_rows[pl.ds(v, 1), :] = jnp.sum(t * zs[v].astype(F32), axis=0, keepdims=True)
+                    scaled.append((k, (t * arep[pl.ds(v, 1), :]).astype(BF16)))
+            for u in range(QUADS):
                 for side in range(2):
-                    v = p + 64 * side
-                    t = dot(kt3[ks[side]], resid[smem[1, v]])
-                    ga_rows[pl.ds(v, 1), :] = jnp.sum(t * zs[v].astype(F32), axis=0, keepdims=True)
-                    scaled.append((t * arep[pl.ds(v, 1), :]).astype(BF16))
-            for u, (p, ks) in enumerate(zip(pairs, which)):
-                gs[pl.ds(pl.multiple_of(p * PITCH, 8), SIDE), :] = dot(
-                    scaled[2 * u], kst_lo[ks[0]]
-                ) + dot(scaled[2 * u + 1], kst_hi[ks[1]])
+                    p = step * QUADS + u + CAP * side
+                    (ka, a), (kb, bb) = scaled[4 * u + 2 * side : 4 * u + 2 * side + 2]
+                    gs[pl.ds(pl.multiple_of(p * PITCH, 8), SIDE), :] = dot(a, kst_lo[ka]) + dot(
+                        bb, kst_hi[kb]
+                    )
             return carry
 
-        def flatten(first):
+        def flatten(part):
             for half in range(2):
                 def grad_body(j, carry, half=half):
                     pair = half * 16 + j
-                    mask = lane_lo(32)
-                    e = gs[pl.ds(first * PITCH + 2 * pair, 32, stride=PITCH), :]
-                    o = gs[pl.ds(first * PITCH + 2 * pair + 1, 32, stride=PITCH), :]
+                    mask = lane_lo(PART)
                     cols = pl.ds(pl.multiple_of(j * 128, 128), 128)
-                    gflat[it, half, first : first + 32, cols] = jnp.where(mask, e, swap(o)).astype(BF16)
-                    gflat[it, half, 64 + first : 96 + first, cols] = jnp.where(
-                        mask, swap(e), o
-                    ).astype(BF16)
+                    for first in (PART * part, CAP + PART * part):
+                        row = first * PITCH + 2 * pair
+                        e = gs[pl.ds(row, PART, stride=PITCH), :]
+                        o = gs[pl.ds(row + 1, PART, stride=PITCH), :]
+                        gflat[it, half, first : first + PART, cols] = jnp.where(
+                            mask, e, swap(o)
+                        ).astype(BF16)
+                        gflat[it, half, 64 + first : 64 + first + PART, cols] = jnp.where(
+                            mask, swap(e), o
+                        ).astype(BF16)
                     return carry
 
                 tiled(16, ROWS, grad_body)
-
-        def give_back(d):
-            part_copy(it, d, other).wait_recv()
-            rows = pl.ds(CAP * d, CAP)
-            gsum[it, rows, :] = (
-                gflat[it, b, rows, :].astype(F32) + gin[it, rows, :].astype(F32)
-            ).astype(BF16)
-            back_copy(it, d).start()
-
-        lax.fori_loop(0, 32 // PAIRS, visit_back, 0)
+            for d in range(4):
+                part_copy(it, d, part, other).start()
+
+        def give_back(part):
+            for d in range(4):
+                part_copy(it, d, part, other).wait_recv()
+                rows = pl.ds(CAP * d + PART * part, PART)
+                gsum[it, rows, :] = (
+                    gflat[it, b, rows, :].astype(F32) + gin[it, rows, :].astype(F32)
+                ).astype(BF16)
+                back_copy(it, d, part).start()
+
+        steps = PART // QUADS
+        lax.fori_loop(0, steps, visit_back, 0)
         flatten(0)
-        for d in (0, 2):
-            part_copy(it, d, other).start()
-        lax.fori_loop(32 // PAIRS, 64 // PAIRS, visit_back, 0)
-        flatten(32)
-        for d in (1, 3):
-            part_copy(it, d, other).start()
-        for d in (0, 2):
-            give_back(d)
+        lax.fori_loop(steps, 2 * steps, visit_back, 0)
+        flatten(1)
+        give_back(0)
         select = jnp.where(
             lax.broadcasted_iota(I32, (8, 256), 1) // SIDE
             == lax.broadcasted_iota(I32, (8, 256), 0),
@@ -544,8 +566,7 @@
             return carry
 
         lax.fori_loop(0, SLOTS // HOME, home_back_body, 0)
-        for d in (1, 3):
-            give_back(d)
+        give_back(1)
 
         for half in range(2):
             def flat_body(j, carry, half=half):
@@ -577,15 +598,19 @@
         home_copy(it).start()
 
         def home_gain(j, carry):
-            cols = pl.ds(pl.multiple_of(j * 256, 256), 256)
+            terms = []
             for half in range(2):
-                carry = carry + lax.dot_general(
-                    bflat[half, 0:48, cols], mq[it, half, :, cols], (((1,), (1,)), ((), ())),
-                    preferred_element_type=F32,
-                )
-            return carry
-
-        gain = lax.fori_loop(0, HALF // 256, home_gain, jnp.zeros((48, SRC), F32))
+                for u in range(2):
+                    cols = pl.ds(pl.multiple_of(j * 1024 + u * 512, 512), 512)
+                    terms.append(
+                        lax.dot_general(
+                            bflat[half, 0:48, cols], mq[it, half, :, cols],
+                            (((1,), (1,)), ((), ())), preferred_element_type=F32,
+                        )
+                    )
+            return carry + ((terms[0] + terms[1]) + (terms[2] + terms[3]))
+
+        gain = lax.fori_loop(0, 2, home_gain, jnp.zeros((48, SRC), F32))
         ga_home[...] = jnp.concatenate(
             [
                 jnp.sum(is_slot * gain[16 * band : 16 * band + 16], axis=0, keepdims=True)
@@ -614,7 +639,8 @@
                 out_a[band] = amp_now[band : band + 1, :]
         home_copy(it).wait_recv()
         for d in range(4):
-            back_copy(it, d).wait_recv()
+            for part in range(2):
+                back_copy(it, d, part).wait_recv()
 
         def update(j, carry):
             cols = pl.ds(pl.multiple_of(j * 128, 128), 128)
@@ -635,7 +661,8 @@
             mine_copy(b).start()
             mine_copy(other).wait_recv()
 
-    pl.run_scoped(with_table, pltpu.SMEM((8, SRC), I32))
+    for it in range(ITERS):
+        one_iteration(it)
 
     for copy in list_copies:
         copy.wait_send()
@@ -644,10 +671,11 @@
         home_copy(it).wait_send()
         for d in range(4):
             amp_copy(it, d).wait_send()
-            vis_copy(it, d).wait_send()
-            fwd_copy(it, d, b).wait_send()
-            part_copy(it, d, other).wait_send()
-            back_copy(it, d).wait_send()
+            for part in range(2):
+                vis_copy(it, d, part).wait_send()
+                fwd_copy(it, d, part, b).wait_send()
+                part_copy(it, d, part, other).wait_send()
+                back_copy(it, d, part).wait_send()
             gain_copy(it, d).wait_send()
 
     @pl.when(x == kind)
@@ -688,6 +716,7 @@
         pltpu.VMEM((SRC, SRC), F32),
         pltpu.VMEM((SRC, SRC), I32),
         pltpu.VMEM((8, SRC), I32),
+        pltpu.SMEM((8, SRC), I32),
         pltpu.VMEM((2, 2, SRC, HALF), BF16),
         pltpu.VMEM((SRC, HALF), F32),
         pltpu.VMEM((2, SRC, HALF), BF16),
@@ -698,7 +727,7 @@
         pltpu.VMEM((SLOTS * PITCH, 128), F32),
         pltpu.VMEM((SLOTS * PITCH, 128), F32),
         pltpu.VMEM((SRC, SIDE, 256), BF16),
-        pltpu.VMEM((130, SIDE, 256), F32),
+        pltpu.VMEM((132, SIDE, 256), F32),
         pltpu.VMEM((SLOTS, SIDE, 256), F32),
         pltpu.VMEM((SLOTS, 256, 256), BF16),
         pltpu.VMEM((SLOTS * PITCH, 128), F32),
@@ -718,8 +747,8 @@
         pltpu.VMEM((2, 4, 8, SRC), F32),
         pltpu.VMEM((8, SRC), F32),
         dma((n_x + 2 * (n_ra // n_x),)), dma((SLOTS,)),
-        dma((2, 4)), dma((2, 2, 4)), dma((2, 2, 4)), dma((2, 2, 4)), dma((2, 1)), dma((2, 2)),
-        dma((2, 2, 4)), dma((2, 2, 4)), dma((2, 2, 4)), dma, dma((3,)),
+        dma((2, 4)), dma((2, 2, 4)), dma((2, 2, 4, 2)), dma((2, 2, 4, 2)), dma((2, 1)), dma((2, 2)),
+        dma((2, 2, 4, 2)), dma((2, 2, 4, 2)), dma((2, 2, 4)), dma, dma((3,)),
     ]
     out_m, out_a = pl.pallas_call(
         functools.partial(deblend, n_ra, n_dec, n_x),
@@ -731,7 +760,7 @@
         out_specs=(vmem, vmem),
         scratch_shapes=scratch,
         compiler_params=pltpu.CompilerParams(
-            collective_id=0, has_side_effects=True, vmem_limit_bytes=60 * 1024 * 1024
+            collective_id=0, has_side_effects=True, vmem_limit_bytes=48 * 1024 * 1024
         ),
         name="deblend",
     )(

time: 83.6 us -> 77.4 us (0.926)
  Pallas kernels: 79.9 us -> 71.2 us
  local copies, waits for them, and re-layouts: 0.01 us -> 3.65 us
  other arithmetic: 2.86 us -> 1.62 us
    pallas_call x1, Pallas kernels: 79.9 us -> 71.2 us  [shards(): pl.pallas_call(functools.partial(deblend, n_ra, n_dec, n_x), out_shape=(j...]
    unnamed x2 -> x14, local copies, waits for them, and re-layouts: 0.01 us -> 3.65 us
    broadcast_in_dim x1, other arithmetic: 2.29 us -> 1.05 us  [shards(): return (out_m[None, None], out_a.reshape(1, 1, 3, SRC))]
where the time goes in v3:
time: 77.4 us; the launch traced here: 77.2 us
  Pallas kernels  71.2 us (92%)
  local copies, waits for them, and re-layouts  3.65 us (5%)
  other arithmetic  1.62 us (2%)
    pallas_call x1, Pallas kernels, shards(): pl.pallas_call(functools.partial(deblend, n_ra, n_dec, n_x), out_shape=(j...  71.2 us
    unnamed x14, local copies, waits for them, and re-layouts  3.65 us

profile of v3, /device:TPU:1, one launch (start us, length us, event | category | flops | bytes accessed | tf_op | source)
XLA Modules:
  0.0 77.2 jit_solution(12141861204542665399)
XLA Ops:
  0.6 0.0 copy-start.3
  0.6 0.0 copy-start.4
  0.7 0.0 copy-start.5
  0.7 0.0 copy-start.6
  0.7 0.6 copy-done.3
  1.3 0.0 copy-done.4
  1.3 0.0 copy-done.5
  1.3 0.0 copy-done.6
  1.3 0.0 copy-start
  1.3 1.2 %copy-done = bf16[1,1,128,4096]{3,2,1,0:T(8,128)(2,1)S(1)} copy-done((bf16[1,1,128,4096]{3,2,1,0:T(8,128)(2,1)S(1)}, bf16[1,1,128,4096]{3,2,1,0:T(8,128)(2,1)}, u32[]{:S(2)}) %copy-start) | copy-done | bytes 1048600
  2.6 0.0 copy-start.1
  2.6 1.0 %copy-done.1 = bf16[1,1,3,16,4096]{4,3,2,1,0:T(8,128)(2,1)S(1)} copy-done((bf16[1,1,3,16,4096]{4,3,2,1,0:T(8,128)(2,1)S(1)}, bf16[1,1,3,16,4096]{4,3,2,1,0:T(8,128)(2,1)}, u32[]{:S(2)}) %copy-start.1) | copy-done | bytes 393240
  3.6 0.0 copy-start.2
  3.6 0.8 copy-done.2
  4.3 71.2 %deblend.1 = (f32[128,2048]{1,0:T(8,128)S(1)}, f32[3,1,128]{2,1,0:T(1,128)S(1)}) custom-call(bf16[128,4096]{1,0:T(8,128)(2,1)S(1)} %bitcast.13, f32[3,1,128]{2,1,0:T(1,128)S(1)} %bitcast.17, s32[5,1,128]{2,1,0:T(1,128)S(1)} %bitcast.16, f32[1,128]{1,0:T(1,128)S(1)} %bitcast.18, f32[1,128]{1,0:T(1,128)S(1)} %bitcast.19, bf16[3,4096]{1,0:T(4,128)(2,1)S(1)} %bitcast.15, ...), custom_call_target="tpu_custom_call" | custom-call | tf_op jit(solution)/shard_map/deblend/pallas_call | solution.py:753
  75.6 1.1 %maximum_bitcast_fusion = f32[1,1,128,2048]{3,2,1,0:T(8,128)} fusion(f32[128,2048]{1,0:T(8,128)S(1)} %get-tuple-element.4), kind=kLoop, calls=%fused_computation | loop fusion | flops 262144 | bytes 2097152 | tf_op jit(solution)/shard_map/broadcast_in_dim | solution.py:771
  76.6 0.6 maximum_bitcast_fusion.1
Async XLA Ops:
  0.6 0.7 copy-start.3
  0.6 0.7 copy-start.4
  0.7 0.7 copy-start.5
  0.7 0.7 copy-start.6
  1.3 1.2 %copy-start = (bf16[1,1,128,4096]{3,2,1,0:T(8,128)(2,1)S(1)}, bf16[1,1,128,4096]{3,2,1,0:T(8,128)(2,1)}, u32[]{:S(2)}) copy-start(bf16[1,1,128,4096]{3,2,1,0:T(8,128)(2,1)} %param.7) | copy-start | bytes 3145732
  2.6 1.0 %copy-start.1 = (bf16[1,1,3,16,4096]{4,3,2,1,0:T(8,128)(2,1)S(1)}, bf16[1,1,3,16,4096]{4,3,2,1,0:T(8,128)(2,1)}, u32[]{:S(2)}) copy-start(bf16[1,1,3,16,4096]{4,3,2,1,0:T(8,128)(2,1)} %param.13) | copy-start | bytes 1179652
  3.6 0.8 copy-start.2

commit v4 on v3

--- a/solution.py
+++ b/solution.py
@@ -100,10 +100,10 @@
     lists8, lists_in, amps, amps_in, amp_now,
     pick_out, pick_back, home_amp, home_back, step_col, entries, table, smem,
     mq, mf, vout, vin, xs, s_lo, s_hi, o_lo, o_hi, zs, pfx, model, resid,
-    b_lo, b_hi, bflat, gs, gflat, gsum, gin, gret, hown, hsend, hin,
+    b_lo, b_hi, bflat, gs, gflat, gsum, gin, gret, hown, hin, amps_twin, twin_back,
     arep, ga_rows, ga_send, ga_ret, ga_home,
     psf_send, psf_recv, list_sem, amp_sem, vis_sem, fwd_sem, mine_sem, home_sem,
-    part_sem, back_sem, gain_sem, table_sem, load_sem,
+    part_sem, back_sem, gain_sem, table_sem, load_sem, twin_sem,
 ):
     r = lax.axis_index("ra")
     c = lax.axis_index("dec")
@@ -235,7 +235,11 @@
         return send(mq.at[1, half], mq.at[1, half], mine_sem, (0,), sibling)
 
     def home_copy(it):
-        return send(hsend.at[it], hin.at[it], home_sem, (it,), sibling)
+        rows = pl.ds(0, 48)
+        return send(bflat.at[other, rows], hin.at[it, rows], home_sem, (it,), sibling)
+
+    def twin_copy(it):
+        return send(amps.at[it], amps_twin.at[it], twin_sem, (it,), sibling)
 
     def part_copy(it, d, part, half):
         rows = pl.ds(CAP * d + PART * part, PART)
@@ -250,6 +254,7 @@
 
     for d in range(4):
         amp_copy(0, d).start()
+    twin_copy(0).start()
 
     for d in range(4):
         row = lists8[d + 1 : d + 2, :]
@@ -284,6 +289,7 @@
     slot0 = lists8[0:1, :]
     is_slot = jnp.where(slot0 == lax.broadcasted_iota(I32, (SLOTS, SRC), 0), 1.0, 0.0)
     bflat[...] = jnp.zeros(bflat.shape, BF16)
+    hin[:, 48:SRC, :] = jnp.zeros((2, SRC - 48, HALF), BF16)
     pfx[0] = jnp.zeros((SIDE, 256), F32)
     for d in range(1, 4):
         pfx[BASE[d]] = jnp.zeros((SIDE, 256), F32)
@@ -588,14 +594,19 @@
 
             tiled(16, ROWS, flat_body)
 
+        home_copy(it).start()
+
         def home_grad(j, carry):
             cols = pl.ds(pl.multiple_of(j * 256, 256), 256)
-            hsend[it, :, cols] = dot(home_back[...], bflat[other, :, cols]).astype(BF16)
             hown[:, cols] = dot(home_back[...], bflat[b, :, cols])
             return carry
 
         tiled(8, 4, home_grad)
-        home_copy(it).start()
+        twin_copy(it).wait_recv()
+        rows = [is_slot * amps_twin[it, band : band + 1, :] for band in range(3)]
+        twin_back[...] = (
+            jnp.concatenate(rows + [jnp.zeros((SRC - 48, SRC), F32)], axis=0).T.astype(BF16)
+        )
 
         def home_gain(j, carry):
             terms = []
@@ -634,17 +645,19 @@
             amps[1] = amp_now[...].astype(BF16).astype(F32)
             for d in range(4):
                 amp_copy(1, d).start()
+            twin_copy(1).start()
         else:
             for band in range(3):
                 out_a[band] = amp_now[band : band + 1, :]
         home_copy(it).wait_recv()
+        home_copy(it).wait_send()
         for d in range(4):
             for part in range(2):
                 back_copy(it, d, part).wait_recv()
 
         def update(j, carry):
             cols = pl.ds(pl.multiple_of(j * 128, 128), 128)
-            grad = hown[:, cols] + hin[it, :, cols].astype(F32)
+            grad = hown[:, cols] + dot(twin_back[...], hin[it, :, cols])
             grad = grad + dot(pick_back[...], gret[it, :, cols])
             fresh = mf[:, cols] - step_col[...] * grad
             if it == 0:
@@ -668,7 +681,7 @@
         copy.wait_send()
     mine_copy(b).wait_send()
     for it in range(ITERS):
-        home_copy(it).wait_send()
+        twin_copy(it).wait_send()
         for d in range(4):
             amp_copy(it, d).wait_send()
             for part in range(2):
@@ -740,7 +753,8 @@
         pltpu.VMEM((2, SRC, HALF), BF16),
         pltpu.VMEM((SRC, HALF), F32),
         pltpu.VMEM((2, SRC, HALF), BF16),
-        pltpu.VMEM((2, SRC, HALF), BF16),
+        pltpu.VMEM((2, 8, SRC), F32),
+        pltpu.VMEM((SRC, SRC), BF16),
         pltpu.VMEM((SRC, 256), F32),
         pltpu.VMEM((SRC, 256), F32),
         pltpu.VMEM((2, 8, SRC), F32),
@@ -748,7 +762,7 @@
         pltpu.VMEM((8, SRC), F32),
         dma((n_x + 2 * (n_ra // n_x),)), dma((SLOTS,)),
         dma((2, 4)), dma((2, 2, 4)), dma((2, 2, 4, 2)), dma((2, 2, 4, 2)), dma((2, 1)), dma((2, 2)),
-        dma((2, 2, 4, 2)), dma((2, 2, 4, 2)), dma((2, 2, 4)), dma, dma((3,)),
+        dma((2, 2, 4, 2)), dma((2, 2, 4, 2)), dma((2, 2, 4)), dma, dma((3,)), dma((2, 2)),
     ]
     out_m, out_a = pl.pallas_call(
         functools.partial(deblend, n_ra, n_dec, n_x),

time: 77.4 us -> 77.6 us (level)
  no operation moved by 1% of the time
where the time goes in v4:
time: 77.6 us; the launch traced here: 77.3 us
  Pallas kernels  71.4 us (92%)
  local copies, waits for them, and re-layouts  3.65 us (5%)
  other arithmetic  1.62 us (2%)
    pallas_call x1, Pallas kernels, shards(): pl.pallas_call(functools.partial(deblend, n_ra, n_dec, n_x), out_shape=(j...  71.4 us
    unnamed x14, local copies, waits for them, and re-layouts  3.65 us

profile of v4, /device:TPU:1, one launch (start us, length us, event | category | flops | bytes accessed | tf_op | source)
XLA Modules:
  0.0 77.3 jit_solution(13115342952299291152)
XLA Ops:
  0.6 0.0 copy-start.3
  0.6 0.0 copy-start.4
  0.7 0.0 copy-start.5
  0.7 0.0 copy-start.6
  0.7 0.6 copy-done.3
  1.3 0.0 copy-done.4
  1.3 0.0 copy-done.5
  1.3 0.0 copy-done.6
  1.3 0.0 copy-start
  1.3 1.2 %copy-done = bf16[1,1,128,4096]{3,2,1,0:T(8,128)(2,1)S(1)} copy-done((bf16[1,1,128,4096]{3,2,1,0:T(8,128)(2,1)S(1)}, bf16[1,1,128,4096]{3,2,1,0:T(8,128)(2,1)}, u32[]{:S(2)}) %copy-start) | copy-done | bytes 1048600
  2.6 0.0 copy-start.1
  2.6 1.0 %copy-done.1 = bf16[1,1,3,16,4096]{4,3,2,1,0:T(8,128)(2,1)S(1)} copy-done((bf16[1,1,3,16,4096]{4,3,2,1,0:T(8,128)(2,1)S(1)}, bf16[1,1,3,16,4096]{4,3,2,1,0:T(8,128)(2,1)}, u32[]{:S(2)}) %copy-start.1) | copy-done | bytes 393240
  3.6 0.0 copy-start.2
  3.6 0.8 copy-done.2
  4.3 71.4 %deblend.1 = (f32[128,2048]{1,0:T(8,128)S(1)}, f32[3,1,128]{2,1,0:T(1,128)S(1)}) custom-call(bf16[128,4096]{1,0:T(8,128)(2,1)S(1)} %bitcast.13, f32[3,1,128]{2,1,0:T(1,128)S(1)} %bitcast.17, s32[5,1,128]{2,1,0:T(1,128)S(1)} %bitcast.16, f32[1,128]{1,0:T(1,128)S(1)} %bitcast.18, f32[1,128]{1,0:T(1,128)S(1)} %bitcast.19, bf16[3,4096]{1,0:T(4,128)(2,1)S(1)} %bitcast.15, ...), custom_call_target="tpu_custom_call" | custom-call | tf_op jit(solution)/shard_map/deblend/pallas_call | solution.py:767
  75.7 1.1 %maximum_bitcast_fusion = f32[1,1,128,2048]{3,2,1,0:T(8,128)} fusion(f32[128,2048]{1,0:T(8,128)S(1)} %get-tuple-element.4), kind=kLoop, calls=%fused_computation | loop fusion | flops 262144 | bytes 2097152 | tf_op jit(solution)/shard_map/broadcast_in_dim | solution.py:785
  76.7 0.6 maximum_bitcast_fusion.1
Async XLA Ops:
  0.6 0.7 copy-start.3
  0.6 0.7 copy-start.4
  0.7 0.7 copy-start.5
  0.7 0.7 copy-start.6
  1.3 1.2 %copy-start = (bf16[1,1,128,4096]{3,2,1,0:T(8,128)(2,1)S(1)}, bf16[1,1,128,4096]{3,2,1,0:T(8,128)(2,1)}, u32[]{:S(2)}) copy-start(bf16[1,1,128,4096]{3,2,1,0:T(8,128)(2,1)} %param.7) | copy-start | bytes 3145732
  2.6 1.0 %copy-start.1 = (bf16[1,1,3,16,4096]{4,3,2,1,0:T(8,128)(2,1)S(1)}, bf16[1,1,3,16,4096]{4,3,2,1,0:T(8,128)(2,1)}, u32[]{:S(2)}) copy-start(bf16[1,1,3,16,4096]{4,3,2,1,0:T(8,128)(2,1)} %param.13) | copy-start | bytes 1179652
  3.6 0.8 copy-start.2
